TPU v7x, 32 devices: a whole 2x2x4 slice. The times are simulated.
32 devices in a mesh: view: 8 (over z, core), slab: 4 (over y, x).
Axes of the slice: x: 2, y: 2, z: 4, core: 2. Of those that a mesh axis runs over, the one named last changes fastest.
Arguments:
- latent: bfloat16 [32, 32, 1024], P(None, 'slab'), may hold values from -6 to 6
- tconv_weight: bfloat16 [32, 32, 8], replicated, may hold values from -1 to 1
- depth_weight: float32 [32, 27], replicated, may hold values from -2 to 2
- point_weight: bfloat16 [4, 32], replicated, may hold values from -1 to 1
- pencil_ids: int32 [8, 1024], P('view'), may hold values from 0 to 4095, as said below
- targets: float32 [8, 3, 1024], P('view', None, 'slab'), may hold values from 0 to 1
Outputs:
- colours: float32 [8, 3, 1024], P('view', None, 'slab')
- latent_grad: float32 [32, 32, 1024], P(None, 'slab')
Inputs may be any that keep to these rules, and one draw needn't show every extreme that they name: `pencil_ids`: within one view group the ids are distinct; every view group names cell 0 and cell 4 * 32 * 32 - 1.
All inputs are finite; a program needn't handle non-finite values.
Results may differ from a plain program's by a relative error of at most 0.005.
Values may be sent and summed in bfloat16 or wider, within the bound.
No kernel may reach another device: no remote copies, remote signals or barrier semaphores. Data moves between devices by JAX's collectives and lax.ppermute only.
A program may use at most 192 MiB of HBM per device.

v0:
```python
import jax
import jax.numpy as jnp
from jax import lax
from jax.sharding import PartitionSpec as P

CX = 32
CY = 32


def padded_2(x, sides, width):
    for axis, dim in sides:
        count, length = (lax.axis_size(axis), x.shape[dim])
        up = [(i, (i + 1) % count) for i in range(count - 1)]
        down = [(j, i) for i, j in up]
        last = lax.slice_in_dim(x, length - width, length, axis=dim)
        initial = lax.slice_in_dim(x, 0, width, axis=dim)
        before = lax.ppermute(last, axis, up)
        after = lax.ppermute(initial, axis, down)
        x = jnp.concatenate([before, x, after], axis=dim)
    return x


def decode_grid(latent, tconv_weight):
    chans = latent.shape[0]
    depth = latent.shape[1]
    grid4 = latent.reshape(chans, depth, CX, CY)
    weight5 = tconv_weight.reshape(chans, chans, 2, 2, 2)
    fine = jnp.einsum("izxy,ioabc->ozaxbyc", grid4, weight5, preferred_element_type=jnp.float32)
    return fine.reshape(chans, 2 * depth, 4 * CX * CY).astype(jnp.bfloat16)


def depthwise_apply(padded, depth_weight, flipped):
    chans = padded.shape[0]
    depth = padded.shape[1] - 2
    grid4 = padded.reshape(chans, depth + 2, 2 * CX, 2 * CY)
    grid4 = jnp.pad(grid4, ((0, 0), (0, 0), (1, 1), (1, 1)))
    total = jnp.zeros((chans, depth, 2 * CX, 2 * CY), jnp.float32)
    for first in range(3):
        for second in range(3):
            for third in range(3):
                coeff = depth_weight[:, 9 * first + 3 * second + third][:, None, None, None]
                if flipped:
                    sa, sb, sc = (2 - first, 2 - second, 2 - third)
                else:
                    sa, sb, sc = (first, second, third)
                total = total + coeff * grid4[
                    :, sa : sa + depth, sb : sb + 2 * CX, sc : sc + 2 * CY
                ].astype(jnp.float32)
    return total.reshape(chans, depth, 4 * CX * CY)


def composite(raw):
    steps_count = raw.shape[1]
    sigma = jax.nn.softplus(raw[0])
    colour = jax.nn.sigmoid(raw[1:4])
    optical = sigma * (1.5 / steps_count)
    before = jnp.cumsum(optical, axis=0) - optical
    weights = jnp.exp(-before) * (1.0 - jnp.exp(-optical))
    return jnp.sum(weights[None] * colour, axis=1)


def on_device(latent, tconv_weight, depth_weight, point_weight, pencil_ids, targets):
    depth = latent.shape[1]
    rim_width = 1
    fine = decode_grid(latent, tconv_weight)
    padded = padded_2(fine, (("slab", 1),), rim_width)
    depth_full = depthwise_apply(padded, depth_weight, False)
    features = jax.nn.silu(depth_full).astype(jnp.bfloat16)
    ids = pencil_ids[0]
    picked = jnp.take(features, ids, axis=2)
    arrived = lax.all_to_all(picked, "slab", split_axis=2, concat_axis=1, tiled=True)
    pencil_raw = jnp.einsum(
        "oc,czp->ozp", point_weight, arrived, preferred_element_type=jnp.float32
    )
    colour, back = jax.vjp(composite, pencil_raw)
    (grad_pencil,) = back(colour - targets[0])
    returned = lax.all_to_all(grad_pencil, "slab", split_axis=1, concat_axis=2, tiled=True)
    grad_raw = jnp.zeros((4, 2 * depth, 4 * CX * CY), jnp.float32).at[:, :, ids].add(returned)
    point_float = point_weight.astype(jnp.float32)
    grad_features = jnp.einsum(
        "oc,ozp->czp", point_float, grad_raw, precision=lax.Precision.HIGHEST
    )
    sig = jax.nn.sigmoid(depth_full)
    grad_depthwise = grad_features * sig * (1.0 + depth_full * (1.0 - sig))
    grad_padded = padded_2(grad_depthwise, (("slab", 1),), 1)
    grad_fine = depthwise_apply(grad_padded, depth_weight, True)
    chans = latent.shape[0]
    grad7 = grad_fine.reshape(chans, depth, 2, CX, 2, CY, 2)
    weight5 = tconv_weight.reshape(chans, chans, 2, 2, 2).astype(jnp.float32)
    local_grad = jnp.einsum("ozaxbyc,ioabc->izxy", grad7, weight5, precision=lax.Precision.HIGHEST)
    local_grad = local_grad.reshape(chans, depth, CX * CY)
    latent_grad = lax.psum(local_grad, "view")
    return (colour[None], latent_grad)


def solution(mesh):
    in_specs = (P(None, "slab", None), P(), P(), P(), P("view", None), P("view", None, "slab"))
    out_specs = (P("view", None, "slab"), P(None, "slab", None))
    return jax.shard_map(
        on_device, mesh=mesh, in_specs=in_specs, out_specs=out_specs, check_vma=False
    )
```

profile of v0, /device:TPU:0, one launch (start us, length us, event | category | flops | bytes accessed | tf_op | source)
XLA Modules:
  0.0 1054.1 jit_solution(4378352441161321782)
XLA Ops:
  10.1 8.9 convert_bitcast_fusion
  19.0 40.9 %copy.106 = bf16[32,8,2,32,2,32,2]{0,6,5,4,3,2,1:T(2,128)(2,1)} copy(bf16[32,8,2,32,2,32,2]{5,0,3,1,6,4,2:T(8,128)(2,1)} %convert_bitcast_fusion) | data formatting | bytes 8388608 | tf_op jit(solution)/shard_map/convert_element_type | solution.py:29
  63.6 5.5 collective-permute-start
  70.0 4.6 collective-permute-done
  75.6 17.1 %pad_maximum_fusion = bf16[32,18,4096]{0,2,1:T(8,128)(2,1)} fusion(bf16[32,1,4096]{0,2,1:T(8,128)(2,1)S(1)} %copy.110, bf16[32,16,4096]{0,2,1:T(8,128)(2,1)} %bitcast.89, bf16[32,1,4096]{0,2,1:T(8,128)(2,1)S(1)} %copy.109), kind=kLoop, calls=%fused_computation.82 | loop fusion | flops 4718592 | bytes 9437184 | tf_op jit(solution)/shard_map/concatenate | solution.py:19
  92.7 257.5 %multiply_add_fusion = f32[32,16,64,64]{0,3,2,1:T(8,128)} fusion(bf16[32,18,64,64]{0,3,2,1:T(8,128)(2,1)} %bitcast.85, f32[32]{0:T(128)S(1)} %get-tuple-element.27, f32[32]{0:T(128)S(1)} %get-tuple-element.28, f32[32]{0:T(128)S(1)} %get-tuple-element.3, f32[32]{0:T(128)S(1)} %get-tuple-element.4, f32[32]{0:T(128)S(1)} %get-tuple-element.5, ...), kind=kLoop, calls=%fused_computation.81 | loop fusion | flops 167772160 | bytes 77598080 | tf_op jit(solution)/shard_map/add | solution.py:46
  350.2 21.7 %copy.133 = f32[32,16,4096]{2,0,1:T(8,128)} copy(f32[32,16,4096]{0,2,1:T(8,128)} %bitcast.87) | data formatting | bytes 16777216 | tf_op jit(solution)/shard_map/reshape | solution.py:49
  371.9 6.1 multiply_convert_fusion
  378.0 18.2 %copy.112 = bf16[32,16,4096]{0,1,2:T(8,128)(2,1)} copy(bf16[32,16,4096]{2,0,1:T(8,128)(2,1)} %multiply_convert_fusion) | data formatting | bytes 8388608 | tf_op jit(solution)/shard_map/convert_element_type | solution.py:68
  396.2 14.1 %gather_fusion = bf16[1024,32,16]{1,2,0:T(8,128)(2,1)} fusion(bf16[32,16,4096]{0,1,2:T(8,128)(2,1)} %copy.112, s32[1024]{0:T(1024)S(1)} %broadcast_clamp_fusion), kind=kCustom, calls=%fused_computation | custom fusion | bytes 2101248 | tf_op jit(solution)/shard_map/jit(_take)/gather | solution.py:70
  410.3 6.6 fusion.78
  416.9 5.6 reshape.151
  422.5 21.0 %all_to_all.36 = bf16[4,2,65536]{2,1,0:T(2,128)(2,1)S(1)} all-to-all(bf16[4,2,65536]{2,1,0:T(2,128)(2,1)S(1)} %reshape.151), channel_id=1, replica_groups=mesh['view'=8,'slab'=4] {'slab'}, dimensions={0} | all-to-all | bytes 2097152 | tf_op jit(solution)/shard_map/all_to_all | solution.py:71
  447.1 4.8 copy.113
  453.6 8.1 all_to_all.37
  466.4 98.0 %scatter_fusion = f32[4,16,4096]{1,0,2:T(4,128)} fusion(f32[4,16,4096]{1,0,2:T(4,128)} %broadcast_in_dim.25, s32[1024]{0:T(1024)S(1)} %bitcast.105, f32[1024,4,16]{2,1,0:T(4,128)S(1)} %bitcast.100), kind=kCustom, calls=%fused_computation.1 | custom fusion | flops 65536 | bytes 790528 | tf_op jit(solution)/shard_map/scatter-add | solution.py:78
  564.5 6.7 copy.117
  571.1 9.1 fusion.52
  584.7 5.9 collective-permute-done.2
  590.7 13.2 %collective-permute-done.3 = f32[32,1,4096]{2,0,1:T(8,128)S(1)} collective-permute-done((f32[32,1,4096]{2,0,1:T(8,128)S(1)}, f32[32,1,4096]{2,0,1:T(8,128)S(1)}, u32[]{:S(2)}, u32[]{:S(2)}) %collective-permute-start.3) | collective-permute-done | bytes 524320 | tf_op jit(solution)/shard_map/ppermute | solution.py:18
  608.0 20.8 %copy.136 = f32[32,18,4096]{0,2,1:T(8,128)} copy(f32[32,18,4096]{2,0,1:T(8,128)} %pad_maximum_fusion.1) | data formatting | bytes 18874368 | tf_op jit(solution)/shard_map/reshape | solution.py:35
  628.9 328.2 %fusion.47 = f32[32,16,64,64]{0,3,2,1:T(8,128)} fusion(f32[32,18,64,64]{0,3,2,1:T(8,128)} %bitcast.84, f32[32]{0:T(128)S(1)} %get-tuple-element.27, f32[32]{0:T(128)S(1)} %get-tuple-element.28, f32[32]{0:T(128)S(1)} %get-tuple-element.3, f32[32]{0:T(128)S(1)} %get-tuple-element.4, f32[32]{0:T(128)S(1)} %get-tuple-element.5, f32[32]{0:T(128)S(1)} %get-tuple-element.6, ...), kind=kLoop, calls=%fused_computation.73 | loop fusion | flops 111149056 | bytes 146804096 | tf_op jit(solution)/shard_map/add | solution.py:46
  957.1 25.1 %fusion.50 = f32[8,32,32,32,1,1,1]{3,2,6,5,4,1,0:T(8,128)} fusion(f32[32,8,2,32,2,32,2]{0,6,5,4,3,2,1:T(2,128)} %bitcast.86, bf16[32,32,2,2,2,1,1]{1,4,3,2,0,6,5:T(2,128)(2,1)S(1)} %bitcast.103), kind=kOutput, calls=%fused_computation.79 | convolution fusion | flops 805306368 | bytes 9453568 | tf_op jit(solution)/shard_map/ozaxbyc,ioabc->izxy/dot_general | solution.py:90
  986.5 58.0 %all-reduce.6.cloned.1.call-done = f32[32,8,1024]{2,1,0:T(8,128)} async-done(((f32[32,8,1024]{2,1,0:T(8,128)}), f32[32,8,1024]{2,1,0:T(8,128)}) %all-reduce.6.cloned.1.call-update) | async-done | bytes 1048592 | tf_op jit(solution)/shard_map/psum | solution.py:92
  (50 shorter events, 33.6 us)
Async XLA Ops:
  7.2 444.7 %copy-start = (bf16[4,32]{1,0:T(4,128)(2,1)S(1)}, bf16[4,32]{1,0:T(4,128)(2,1)}, u32[]{:S(2)}) copy-start(bf16[4,32]{1,0:T(4,128)(2,1)} %param.9) | copy-start | bytes 772
  7.2 61.9 %copy-start.4 = (s32[1,1024]{1,0:T(1,128)S(1)}, s32[1,1024]{1,0:T(1,128)}, u32[]{:S(2)}) copy-start(s32[1,1024]{1,0:T(1,128)} %param.10) | copy-start | bytes 12292
  7.2 62.0 %copy-start.2 = (f32[32,27]{1,0:T(8,128)S(1)}, f32[32,27]{1,0:T(8,128)}, u32[]{:S(2)}) copy-start(f32[32,27]{1,0:T(8,128)} %param.8) | copy-start | bytes 10372
  7.2 1037.3 %all-reduce.6.cloned.1.call-start = ((), (), s32[]{:S(2)}) async-start(), calls=%async_computation.2 | async-start | bytes 2097152 | tf_op jit(solution)/shard_map/psum | solution.py:92
  62.0 13.2 %collective-permute-start.1 = (bf16[32,1,4096]{2,0,1:T(8,128)(2,1)S(1)}, bf16[32,1,4096]{2,0,1:T(8,128)(2,1)S(1)}, u32[]{:S(2)}, u32[]{:S(2)}) collective-permute-start(bf16[32,1,4096]{2,0,1:T(8,128)(2,1)S(1)} %copy.108), channel_id=1, source_target_pairs={{1,0},{2,1},{3,2},{5,4},{6,5},{7,6},{9,8},{10,9},{11,10},{13,12},{... | collective-permute-start | bytes 786440 | tf_op jit(solution)/shard_map/ppermute | solution.py:18
  63.6 11.0 %collective-permute-start = (bf16[32,1,4096]{2,0,1:T(8,128)(2,1)S(1)}, bf16[32,1,4096]{2,0,1:T(8,128)(2,1)S(1)}, u32[]{:S(2)}, u32[]{:S(2)}) collective-permute-start(bf16[32,1,4096]{2,0,1:T(8,128)(2,1)S(1)} %copy.107), channel_id=1, source_target_pairs={{0,1},{1,2},{2,3},{4,5},{5,6},{6,7},{8,9},{9,10},{10,11},{12,13},{... | collective-permute-start | bytes 786440 | tf_op jit(solution)/shard_map/ppermute | solution.py:17
  371.9 80.6 %copy-start.5 = (f32[1,3,256]{2,0,1:T(1,128)S(1)}, f32[1,3,256]{2,0,1:T(1,128)}, u32[]{:S(2)}) copy-start(f32[1,3,256]{2,0,1:T(1,128)} %param.11) | copy-start | bytes 9220
  580.3 10.3 collective-permute-start.2
  583.2 20.6 %collective-permute-start.3 = (f32[32,1,4096]{2,0,1:T(8,128)S(1)}, f32[32,1,4096]{2,0,1:T(8,128)S(1)}, u32[]{:S(2)}, u32[]{:S(2)}) collective-permute-start(f32[32,1,4096]{2,0,1:T(8,128)S(1)} %get-tuple-element.32), channel_id=1, source_target_pairs={{1,0},{2,1},{3,2},{5,4},{6,5},{7,6},{9,8},{10,9},{11,10},{13,12},{... | collective-permute-start | bytes 1572872 | tf_op jit(solution)/shard_map/ppermute | solution.py:18
  628.9 328.2 %copy-start.3 = (bf16[32,32,8]{1,2,0:T(8,128)(2,1)S(1)}, bf16[32,32,8]{1,2,0:T(8,128)(2,1)}, u32[]{:S(2)}) copy-start(bf16[32,32,8]{1,2,0:T(8,128)(2,1)} %param.7) | copy-start | bytes 49156
  957.1 89.7 %copy-start.1 = (bf16[4,32]{1,0:T(4,128)(2,1)S(1)}, bf16[4,32]{1,0:T(4,128)(2,1)}, u32[]{:S(2)}) copy-start(bf16[4,32]{1,0:T(4,128)(2,1)} %param.9) | copy-start | bytes 772
Sparse Core Ops, SparseCore 0:
  986.1 58.3 all-reduce.5
where the time goes:
time: 1060 us; the launch traced here: 1050 us
  other arithmetic  719 us (68%)
  local copies, waits for them, and re-layouts  155 us (15%)
  waiting for transfers between devices  81.7 us (8%)
  matrix products  43.4 us (4%)
  blocking collectives  29.2 us (3%)
  between operations  14.8 us (1%)
  starting transfers between devices  11.2 us (1%)
    add x2, other arithmetic, depthwise_apply(): total + coeff * grid4[:, sa:sa + depth, sb:sb + 2 * CX, sc:sc + 2 * CY].a...  586 us
    scatter-add x1, other arithmetic, on_device(): jnp.zeros((4, 2 * depth, 4 * CX * CY), jnp.float32).at[:, :, ids]  98 us
    psum x1, waiting for transfers between devices, on_device(): latent_grad = lax.psum(local_grad, 'view')  58 us
    convert_element_type x1, local copies, waits for them, and re-layouts, decode_grid(): return fine.reshape(chans, 2 * depth, 4 * CX * CY).astype(jnp.bfloat16)  40.9 us
    dot_general x1, matrix products, on_device(): jnp.einsum('ozaxbyc,ioabc->izxy', grad7, weight5, precision=lax.Precision...  25.1 us
    reshape x1, local copies, waits for them, and re-layouts, depthwise_apply(): return total.reshape(chans, depth, 4 * CX * CY)  21.7 us
    concatenate x2, other arithmetic, padded_2(): x = jnp.concatenate([before, x, after], axis=dim)  21.3 us
  transfers between devices with their start and end apart: 5, of which 4 were waited for; matrix products, arithmetic and copies ran while one was open for 0% of the time, Pallas kernels for 0%

commit v1 on v0

v1 whole, which is shorter than its diff:
```python
import functools

import jax
import jax.numpy as jnp
from jax import lax
from jax.experimental import pallas as pl
from jax.experimental.pallas import tpu as pltpu
from jax.sharding import PartitionSpec as P

CX = 32
CY = 32
F32 = jnp.float32
BF16 = jnp.bfloat16
VMEM_LIMIT = 24 * 1024 * 1024
VM = pl.BlockSpec(memory_space=pltpu.VMEM)
SM = pl.BlockSpec(memory_space=pltpu.SMEM)


def rows_of(split):
    if split == 1:
        return CX
    return min(CX, -(-(CX // split + 1) // 4) * 4)


def lane_shift(x, amount, y):
    width = x.shape[-1]
    moved = pltpu.roll(x, (-amount) % width, 1)
    if amount == 1:
        keep = y < CY - 1
    elif amount == -1:
        keep = y > 0
    else:
        lane = lax.broadcasted_iota(jnp.int32, x.shape, 1)
        keep = lane < width - CY if amount > 0 else lane >= CY
    return jnp.where(keep, moved, 0.0)


def thirds(x):
    high = x.astype(BF16)
    rest = x - high.astype(F32)
    mid = rest.astype(BF16)
    low = (rest - mid.astype(F32)).astype(BF16)
    return jnp.concatenate([high, mid, low], axis=0)


def softplus(x):
    return jnp.maximum(x, 0.0) + jnp.log1p(jnp.exp(-jnp.abs(x)))


def swap(x):
    return pltpu.roll(x, 4, 0)


def spread(x, put):
    chans, width = x.shape
    lane = lax.broadcasted_iota(jnp.int32, (chans, width), 1)

    def keep(inside):
        return jnp.where(inside, 1.0, 0.0).astype(BF16)

    before = pltpu.roll(x * keep(lane % CY != CY - 1), 1, 1)
    after = pltpu.roll(x * keep(lane % CY != 0), width - 1, 1)
    for j, by_y in enumerate((before, x, after)):
        put(chans * j, pltpu.roll(by_y * keep(lane < width - CY), CY, 1))
        put(chans * (3 + j), by_y)
        put(chans * (6 + j), pltpu.roll(by_y * keep(lane >= CY), width - CY, 1))


def composed(taps_ref, weight, e):
    total = None
    for a in range(2):
        for b in range(2):
            for c in range(2):
                d = (a + 2 - e[0], b + 2 - e[1], c + 2 - e[2])
                if min(d) >= 0 and max(d) <= 2:
                    term = weight(9 * d[0] + 3 * d[1] + d[2]) * taps_ref[4 * a + 2 * b + c]
                    total = term if total is None else total + term
    return total


def near(parity):
    return (-1, 0) if parity == 0 else (0, 1)


def decode_pair(layers, wide_ref, point, slope_ref, raw_ref, k):
    chans = wide_ref.shape[1] // 4
    features = []
    for b in range(2):
        for c in range(2):
            around = jnp.concatenate(
                [
                    layers[j](chans * (3 * (nx + 1) + ny + 1))
                    for j in range(2)
                    for nx in near(b)
                    for ny in near(c)
                ],
                axis=0,
            )
            dw = jnp.dot(wide_ref[2 * b + c], around, preferred_element_type=F32)
            dw = dw[: 2 * chans] + dw[2 * chans :]
            sig = jax.nn.sigmoid(dw)
            silu = dw * sig
            row = 2 * chans * (2 * b + c)
            slope_ref[k, row : row + 2 * chans, :] = silu + sig * (1.0 - silu)
            features.append(silu.astype(BF16))
    raw_ref[k] = jnp.dot(point, jnp.concatenate(features, axis=0), preferred_element_type=F32)


def weight_kernel(taps_ref, depth_ref, wide_ref, full_ref):
    chans = taps_ref.shape[1]
    columns = [jnp.broadcast_to(depth_ref[:, i : i + 1], (chans, chans)) for i in range(27)]
    for b in range(2):
        for c in range(2):
            for first in range(2):
                for j in range(2):
                    for nx in near(b):
                        for ny in near(c):
                            e = (2 - 2 * j + first, b - 2 * nx + 1, c - 2 * ny + 1)
                            at = chans * (4 * j + 2 * (nx - near(b)[0]) + ny - near(c)[0])
                            full_ref[2 * b + c, chans * first : chans * (first + 1), at : at + chans] = composed(
                                taps_ref, lambda i: columns[i], e
                            )
    high = full_ref[...].astype(BF16)
    wide_ref[:, : 2 * chans, :] = high
    wide_ref[:, 2 * chans :, :] = (full_ref[...] - high.astype(F32)).astype(BF16)


def turn_kernel(taps_ref, depth_ref, wide_ref, full_ref):
    chans = taps_ref.shape[1]
    full_ref[...] = jnp.zeros_like(full_ref)
    columns = [jnp.broadcast_to(depth_ref[:, i : i + 1], (chans, chans)) for i in range(27)]
    for b in range(2):
        for n in range(2):
            nx = n - b
            for ny in (-1, 0, 1):
                col = chans * (3 * n + ny + 1)
                for j in range(4):
                    for c in range(2):
                        e = (j, 2 * nx + b + 1, 2 * ny + c + 1)
                        if 0 <= e[2] < 4:
                            row = chans * (4 * (j // 2) + 2 * c + j % 2)
                            full_ref[b, row : row + chans, col : col + chans] = composed(
                                taps_ref, lambda i: columns[i], e
                            )
        wide_ref[b] = full_ref[b].T[: 6 * chans].astype(BF16)


def inner_kernel(lat_ref, wide_ref, point_ref, away_ref, raw_ref, edge_ref, x9_ref, slope_ref, sems):
    layers, chans, width = lat_ref.shape


    def layer(k):
        def put(at, block):
            x9_ref[k, at : at + chans, :] = block

        spread(lat_ref[k], put)

    layer(0)
    for k in range(layers - 1):
        layer(k + 1)
        around = [lambda at, j=j: x9_ref[k + j, at : at + chans, :] for j in range(2)]
        decode_pair(around, wide_ref, point_ref[...], slope_ref, raw_ref, k)
        pltpu.make_async_copy(slope_ref.at[k], away_ref.at[k], sems.at[k]).start()
    edge_ref[0] = x9_ref[0]
    edge_ref[1] = x9_ref[layers - 1]
    for k in range(layers - 1):
        pltpu.make_async_copy(slope_ref.at[k], away_ref.at[k], sems.at[k]).wait()


def outer_kernel(
    scale, where_ref, one_ref, two_ref, edge_ref, wide_ref, point_ref, inner_ref,
    slope_ref, raw_ref, tot_ref, x9_ref,
):
    slab, slabs = where_ref[0], where_ref[3]
    width = one_ref.shape[1]
    chans = edge_ref.shape[1] // 9
    pairs = inner_ref.shape[0] + 2
    even = lax.rem(slab, 2) == 0
    one, two = one_ref[0:chans, :], two_ref[0:chans, :]
    low = jnp.where(slab == 0, 0.0, jnp.where(even, two, one))
    high = jnp.where(slab == slabs - 1, 0.0, jnp.where(even, one, two))
    for k, x in ((0, low), (1, high)):

        def put(at, block, k=k):
            x9_ref[k, at : at + chans, :] = block

        spread(x.astype(BF16), put)
        layers = [lambda at, k=k: x9_ref[k, at : at + chans, :], lambda at, k=k: edge_ref[k, at : at + chans, :]]
        decode_pair(layers if k == 0 else layers[::-1], wide_ref, point_ref[...], slope_ref, raw_ref, k)
    second = lax.broadcasted_iota(jnp.int32, (8, width), 0) >= 4
    before = jnp.zeros((8, width), F32)
    colour = [jnp.zeros((8, width), F32) for _ in range(3)]
    for k in range(pairs):
        raw = raw_at(raw_ref, inner_ref, k)
        tau = softplus(raw[0:8]) * scale
        if k == 0:
            tau = jnp.where(second, tau, 0.0)
        if k == pairs - 1:
            tau = jnp.where(second, 0.0, tau)
        other = swap(tau)
        weight = jnp.exp(-(before + jnp.where(second, other, 0.0))) * (1.0 - jnp.exp(-tau))
        before = before + (tau + other)
        for o in range(3):
            colour[o] = colour[o] + weight * jax.nn.sigmoid(raw[8 * o + 8 : 8 * o + 16])
    colour = [c + swap(c) for c in colour]
    tot_ref[0:8, :] = jnp.where(second, colour[0], before)
    tot_ref[8:16, :] = jnp.where(second, colour[2], colour[1])


def raw_at(outer_ref, inner_ref, k):
    last = inner_ref.shape[0] + 1
    if k == 0:
        return outer_ref[0]
    if k == last:
        return outer_ref[1]
    return inner_ref[k - 1]


def cell_of(ids):
    fine_x, fine_y = ids // (2 * CY), ids % (2 * CY)
    return (fine_x // 2) * CY + fine_y // 2, (fine_x % 2) * 2 + fine_y % 2


def target_kernel(where_ref, tot_ref, own_ref, other_ref, msg_ref):
    width = tot_ref.shape[1]
    start = where_ref[1]
    msg_ref[0:16, :] = tot_ref[...]
    count = own_ref.shape[1]
    row = lax.broadcasted_iota(jnp.int32, (16, count), 0)
    cells = lax.broadcasted_iota(jnp.int32, (count, width), 1)
    total = jnp.zeros((48, width), F32)
    for ref in (own_ref, other_ref):
        for j in range(ref.shape[0] // 4):
            block = ref[4 * j : 4 * j + 4, :]
            cell, part = cell_of(block[3:4, :].astype(jnp.int32))
            value = jnp.where(row < 4, 1.0, jnp.where(row < 8, block[0:1, :], jnp.where(row < 12, block[1:2, :], block[2:3, :])))
            value = jnp.where(row % 4 == part, value, 0.0)
            column = jnp.broadcast_to(cell - start, (8, count)).astype(F32).T[:, 0:1].astype(jnp.int32)
            hot = jnp.where(cells == column, 1.0, 0.0).astype(BF16)
            total = total + jnp.dot(thirds(value), hot, preferred_element_type=F32)
    msg_ref[16:32, :] = total[0:16] + (total[16:32] + total[32:48])


def back_kernel(scale, where_ref, *refs):
    (*msg_refs, inner_ref, outer_ref, away_ref, slope2_ref, wide_ref, point_ref, near_ref) = refs[:-8]
    grad_ref, colour_ref, gdw_ref, e_ref, w_ref, tile_ref, slope_ref, sems = refs[-8:]
    slab, start, own_start = where_ref[0], where_ref[1], where_ref[2]
    slabs = len(msg_refs)
    inner, _, width = inner_ref.shape
    pairs = inner + 2
    chans = slope_ref.shape[1] // 8
    own_width = grad_ref.shape[1]
    second = lax.broadcasted_iota(jnp.int32, (8, width), 0) >= 4
    for k in range(inner):
        pltpu.make_async_copy(away_ref.at[k], slope_ref.at[k], sems.at[k]).start()

    def both(x):
        other = swap(x)
        return jnp.where(second, other, x), jnp.where(second, x, other)

    totals, colours, hits = [], [], None
    for ref in msg_refs:
        tau_total, c0 = both(ref[0:8, :])
        c1, c2 = both(ref[8:16, :])
        totals.append(tau_total)
        colours.append((c0, c1, c2))
        here = (ref[16:24, :], ref[24:32, :])
        hits = here if hits is None else (hits[0] + here[0], hits[1] + here[1])
    index = [lax.rem(slab - k + slabs, slabs) for k in range(slabs)]
    full = [jnp.zeros((8, width), F32) for _ in range(3)]
    after = [jnp.zeros((8, width), F32) for _ in range(3)]
    prefix = None
    for k in range(slabs):
        ahead = jnp.zeros((8, width), F32)
        for other in range(slabs):
            if other != k:
                ahead = ahead + jnp.where(index[other] < index[k], totals[other], 0.0)
        if k == 0:
            prefix = ahead
        through = jnp.exp(-ahead)
        for o in range(3):
            part = through * colours[k][o]
            full[o] = full[o] + part
            if k:
                after[o] = after[o] + jnp.where(index[k] > slab, part, 0.0)
    number, t0 = both(hits[0])
    t1, t2 = both(hits[1])
    pull = [number * full[o] - t for o, t in enumerate((t0, t1, t2))]

    tau0 = softplus(outer_ref[0, 0:8, :]) * scale
    before = -both(tau0)[0]
    for k in range(pairs):
        tau = softplus(raw_at(outer_ref, inner_ref, k)[0:8]) * scale
        other = swap(tau)
        through = jnp.exp(-(prefix + (before + jnp.where(second, other, 0.0))))
        before = before + (tau + other)
        left = jnp.exp(-tau)
        w_ref[k, 0:8, :] = through * (1.0 - left)
        w_ref[k, 8:16, :] = through * left
    last = pairs - 1
    for o in range(3):
        e = w_ref[last, 0:8, :] * jax.nn.sigmoid(outer_ref[1, 8 * o + 8 : 8 * o + 16, :])
        after[o] = after[o] - both(e)[1]
    for k in range(pairs - 1, -1, -1):
        weight, later = w_ref[k, 0:8, :], w_ref[k, 8:16, :]
        raw = raw_at(outer_ref, inner_ref, k)
        total = jnp.zeros((8, width), F32)
        outside = None
        if k == 0:
            outside = jnp.logical_and(jnp.logical_not(second), slab == 0)
        if k == last:
            outside = jnp.logical_and(second, slab == slabs - 1)
        for o in range(3):
            rgb = jax.nn.sigmoid(raw[8 * o + 8 : 8 * o + 16])
            e = weight * rgb
            other = swap(e)
            rest = after[o] + jnp.where(second, 0.0, other)
            after[o] = after[o] + (e + other)
            total = total + pull[o] * (later * rgb - rest)
            grad = pull[o] * (e * (1.0 - rgb))
            if outside is not None:
                grad = jnp.where(outside, 0.0, grad)
            e_ref[k, 8 * o + 8 : 8 * o + 16, :] = grad
        grad = total * (scale * jax.nn.sigmoid(raw[0:8]))
        if outside is not None:
            grad = jnp.where(outside, 0.0, grad)
        e_ref[k, 0:8, :] = grad

    count = near_ref.shape[1]
    cell, part = cell_of(near_ref[...])
    cell = cell - own_start
    mine = jnp.logical_and(cell >= 0, cell < own_width)
    cell = jnp.where(mine, cell + (own_start - start), -1)
    hot = jnp.where(lax.broadcasted_iota(jnp.int32, (width, count), 0) == cell, 1.0, 0.0).astype(BF16)
    rows = jnp.concatenate(
        [jnp.where(second, full[1], full[0]), jnp.where(second, full[2], full[2])], axis=0
    )
    found = jnp.dot(thirds(rows), hot, preferred_element_type=F32)
    found = found[0:16] + (found[16:32] + found[32:48])
    row = lax.broadcasted_iota(jnp.int32, (16, count), 0)
    found = jnp.where(row % 4 == part, found, 0.0)
    for o in range(3):
        colour_ref[o : o + 1, :] = jnp.sum(found[4 * o : 4 * o + 4], axis=0, keepdims=True)

    def pair(k):
        if 0 < k < last:
            pltpu.make_async_copy(away_ref.at[k - 1], slope_ref.at[k - 1], sems.at[k - 1]).wait()
            slope = slope_ref[k - 1]
        else:
            slope = slope2_ref[k // last]
        grad_features = jnp.dot(point_ref[...], thirds(e_ref[k]), preferred_element_type=F32)
        gdw_ref[k] = (grad_features * slope).astype(BF16)

    y = lax.broadcasted_iota(jnp.int32, (chans, width), 1) % CY
    low = own_start == start
    for k in (0, last, *range(1, last)):
        pair(k)
    for z in range(pairs - 1):
        every = []
        for b in range(2):
            at = 4 * chans * b
            around = gdw_ref[z : z + 2, at : at + 4 * chans, :].reshape(8 * chans, width)
            every.append(jnp.dot(wide_ref[b], around, preferred_element_type=F32))
        total = None
        for j in range(3):
            at = chans * j
            line = every[0][at : at + chans] + every[1][at + 3 * chans : at + 4 * chans]
            line = line + lane_shift(every[1][at : at + chans], -CY, y)
            line = line + lane_shift(every[0][at + 3 * chans : at + 4 * chans], CY, y)
            if j != 1:
                line = lane_shift(line, j - 1, y)
            total = line if total is None else total + line
        if own_width < width:
            total = jnp.where(low, total[:, :own_width], total[:, width - own_width :])
        for t in range(own_width // 128):
            tile_ref[t, pl.ds(z, chans, stride=pairs - 1), :] = total[:, 128 * t : 128 * t + 128]
    for t in range(own_width // 128):
        grad_ref[:, 128 * t : 128 * t + 128] = tile_ref[t]


def call(kernel, outs, scratch, operands, smem, away_in=None, away_out=None):
    operands = list(operands)
    specs = [SM] * smem + [VM] * (len(operands) - smem)
    out_specs = [VM] * len(outs)
    shapes = [jax.ShapeDtypeStruct(s, t) for s, t in outs]
    if away_in is not None:
        operands[away_in] = pltpu.with_memory_space_constraint(operands[away_in], pltpu.HBM)
        specs[away_in] = pl.BlockSpec(memory_space=pltpu.HBM)
    if away_out is not None:
        shapes[away_out] = pltpu.HBM(*outs[away_out])
        out_specs[away_out] = pl.BlockSpec(memory_space=pltpu.HBM)
    return pl.pallas_call(
        kernel,
        out_shape=shapes,
        in_specs=specs,
        out_specs=out_specs,
        scratch_shapes=[pltpu.VMEM(*x) if isinstance(x, tuple) else x for x in scratch],
        compiler_params=pltpu.CompilerParams(vmem_limit_bytes=VMEM_LIMIT),
    )(*operands)


def on_device(latent, tconv_weight, depth_weight, point_weight, pencil_ids, targets):
    chans, depth, cells = latent.shape
    view, slab = lax.axis_index("view"), lax.axis_index("slab")
    views, slabs = lax.axis_size("view"), lax.axis_size("slab")
    count = targets.shape[2]
    split = 2 if views % 2 == 0 else 1
    rows = rows_of(split)
    width, own_width = rows * CY, cells // split
    half = view % split
    start = half * (cells - width)
    own_start = half * own_width
    where = jnp.stack([slab, start, own_start, slabs]).astype(jnp.int32)
    scale = 1.5 / (2 * depth * slabs)

    window = lax.dynamic_slice_in_dim(jnp.transpose(latent, (1, 0, 2)), start, width, axis=2)
    even = slab % 2 == 0
    first, last = window[0].astype(F32), window[depth - 1].astype(F32)
    ids = lax.dynamic_slice_in_dim(pencil_ids, slab * count, count, axis=1)
    blocks = jnp.concatenate([targets[0], ids.astype(F32)], axis=0)

    def widened(x):
        return jnp.pad(x, ((0, 0), (0, width - count)))

    def send(x, mask, partner):
        pairs = [(v * slabs + s, (v ^ mask) * slabs + partner(s)) for v in range(views) for s in range(slabs)]
        return lax.ppermute(x, ("view", "slab"), pairs)

    taps = jnp.transpose(tconv_weight.astype(F32), (2, 1, 0))
    eye = jnp.eye(8, dtype=BF16)
    point = point_weight[:, None, None, :] * eye[None, :, :, None]
    point = jnp.transpose(point.reshape(4, 8, 2, 4, chans), (0, 1, 3, 2, 4)).reshape(32, 8 * chans)
    point_back = jnp.tile(point.T, (1, 3))
    (wide,) = call(
        weight_kernel,
        [((4, 4 * chans, 8 * chans), BF16)],
        [((4, 2 * chans, 8 * chans), F32)],
        (taps, depth_weight),
        0,
    )
    (turned,) = call(
        turn_kernel,
        [((2, 6 * chans, 8 * chans), BF16)],
        [((2, 8 * chans, 8 * chans), F32)],
        (taps, depth_weight),
        0,
    )

    masks = [split << k for k in range((views // split).bit_length() - 1)]
    one = send(
        jnp.concatenate([jnp.where(even, last, first), widened(blocks)], axis=0),
        masks[0] if masks else 0,
        lambda s: (s + 1 - 2 * (s % 2)) % slabs,
    )
    one, wide, turned = lax.optimization_barrier((one, wide, turned))
    if masks:
        blocks = jnp.concatenate([blocks, one[chans:, :count]], axis=0)
    two = send(
        jnp.concatenate([jnp.where(even, first, last), widened(blocks)], axis=0),
        masks[1] if len(masks) > 1 else 0,
        lambda s: (s + 2 * (s % 2) - 1) % slabs,
    )
    inner = depth - 1
    slope, raw, edge = call(
        inner_kernel,
        [((inner, 8 * chans, width), F32), ((inner, 32, width), F32), ((2, 9 * chans, width), BF16)],
        [
            ((depth, 9 * chans, width), BF16),
            ((inner, 8 * chans, width), F32),
            pltpu.SemaphoreType.DMA((inner,)),
        ],
        (window, wide, point),
        0,
        away_out=0,
    )
    two, raw, edge = lax.optimization_barrier((two, raw, edge))
    if len(masks) > 1:
        blocks = jnp.concatenate([blocks, two[chans:, :count]], axis=0)
    for mask in masks[2:]:
        blocks = jnp.concatenate([blocks, send(blocks, mask, lambda s: s)], axis=0)
    own_blocks = blocks
    if split == 2:
        pairing = [(i, i ^ 1) for i in range(views)]
        other_blocks = lax.ppermute(own_blocks, "view", pairing)
        near_ids = jnp.concatenate([ids, other_blocks[3:4].astype(jnp.int32)], axis=1)
    else:
        other_blocks, near_ids = own_blocks[:0], ids
    slope2, raw2, tot = call(
        functools.partial(outer_kernel, scale),
        [((2, 8 * chans, width), F32), ((2, 32, width), F32), ((16, width), F32)],
        [((2, 9 * chans, width), BF16)],
        (where, one, two, edge, wide, point, raw),
        1,
    )
    (message,) = call(target_kernel, [((32, width), F32)], [], (where, tot, own_blocks, other_blocks), 1)
    messages = [message]
    for k in range(1, slabs):
        messages.append(lax.ppermute(message, "slab", [(i, (i + k) % slabs) for i in range(slabs)]))
    grad, found = call(
        functools.partial(back_kernel, scale),
        [((chans * depth, own_width), F32), ((3, split * count), F32)],
        [
            ((inner + 2, 8 * chans, width), BF16),
            ((inner + 2, 32, width), F32),
            ((inner + 2, 16, width), F32),
            ((own_width // 128, chans * depth, 128), F32),
            ((inner, 8 * chans, width), F32),
            pltpu.SemaphoreType.DMA((inner,)),
        ],
        (where, *messages, raw, raw2, slope, slope2, turned, point_back, near_ids),
        1,
        away_in=slabs + 3,
    )
    colour = found[:, :count]
    if split == 2:
        other = lax.ppermute(grad, "view", pairing)
        colour = colour + lax.ppermute(found[:, count:], "view", pairing)
        grad = jnp.where(
            half == 0,
            jnp.concatenate([grad, other], axis=1),
            jnp.concatenate([other, grad], axis=1),
        )
    return (colour[None], grad.reshape(chans, depth, cells))


def solution(mesh):
    in_specs = (P(None, "slab", None), P(), P(), P(), P("view", None), P("view", None, "slab"))
    out_specs = (P("view", None, "slab"), P(None, "slab", None))
    return jax.shard_map(
        on_device, mesh=mesh, in_specs=in_specs, out_specs=out_specs, check_vma=False
    )
```

time: 1060 us -> 39.4 us (0.04)
  other arithmetic: 719 us -> 2.82 us
  local copies, waits for them, and re-layouts: 155 us -> 3.59 us
  waiting for transfers between devices: 81.7 us -> 4.63 us
  matrix products: 43.4 us -> 0 us
  blocking collectives: 29.2 us -> 0 us
  between operations: 14.8 us -> 0.83 us
  Pallas kernels: 0 us -> 13.7 us
    add x2 -> x0, other arithmetic: 586 us -> none  [depthwise_apply(): total + coeff * grid4[:, sa:sa + depth, sb:sb + 2 * CX, sc:sc + 2 * CY].a...]
    scatter-add x1 -> x0, other arithmetic: 98 us -> none  [on_device(): jnp.zeros((4, 2 * depth, 4 * CX * CY), jnp.float32).at[:, :, ids]]
    convert_element_type x2 -> x0, local copies, waits for them, and re-layouts: 59.1 us -> none  [the longest x1 40.9 us: decode_grid(): return fine.reshape(chans, 2 * depth, 4 * CX * CY).astype(jnp.bfloat16)]
    psum x1 -> x0, waiting for transfers between devices: 58 us -> none  [on_device(): latent_grad = lax.psum(local_grad, 'view')]
    reshape x4 -> x0, local copies, waits for them, and re-layouts: 49.1 us -> none  [the longest x1 21.7 us: depthwise_apply(): return total.reshape(chans, depth, 4 * CX * CY)]
    dot_general x4 -> x0, matrix products: 43.4 us -> none  [the longest x1 25.1 us: on_device(): jnp.einsum('ozaxbyc,ioabc->izxy', grad7, weight5, precision=lax.Precision...]
    all_to_all x2 -> x0, blocking collectives: 29.2 us -> none  [the longest x1 21 us: on_device(): lax.all_to_all(picked, 'slab', split_axis=2, concat_axis=1, tiled=True)]
    concatenate x2 -> x6, other arithmetic: 21.3 us -> 0.06 us  [the longest x1 0.01 us: on_device(): blocks = jnp.concatenate([blocks, two[chans:, :count]], axis=0)]
  transfers between devices with their start and end apart: 5 -> 8, of which waited for: 4 -> 5; matrix products, arithmetic and copies ran while one was open for 0% -> 7% of each run, Pallas kernels for 0% -> 17%
where the time goes in v1:
time: 39.4 us; the launch traced here: 39 us
  Pallas kernels  13.7 us (35%)
  starting transfers between devices  13.5 us (34%)
  waiting for transfers between devices  4.63 us (12%)
  local copies, waits for them, and re-layouts  3.59 us (9%)
  other arithmetic  2.82 us (7%)
  between operations  0.83 us (2%)
    pallas_call x6, Pallas kernels, call(): pl.pallas_call(kernel, out_shape=shapes, in_specs=specs, out_specs=out_sp...  13.7 us
    ppermute x2, starting transfers between devices, send(): return lax.ppermute(x, ('view', 'slab'), pairs)  8.73 us
    ppermute x3, starting transfers between devices, on_device(): lax.ppermute(message, 'slab', [(i, (i + k) % slabs) for i in range(slabs)])  4.14 us
    unnamed x8, local copies, waits for them, and re-layouts  3.32 us
    ppermute x3, waiting for transfers between devices, on_device(): lax.ppermute(message, 'slab', [(i, (i + k) % slabs) for i in range(slabs)])  3.14 us
    ppermute x1, waiting for transfers between devices, on_device(): colour = colour + lax.ppermute(found[:, count:], 'view', pairing)  1.4 us
    select_n x1, other arithmetic, on_device(): jnp.where(half == 0, jnp.concatenate([grad, other], axis=1), jnp.concaten...  1.15 us
    mul x1, other arithmetic, on_device(): point = point_weight[:, None, None, :] * eye[None, :, :, None]  0.8 us
  transfers between devices with their start and end apart: 8, of which 5 were waited for; matrix products, arithmetic and copies ran while one was open for 7% of the time, Pallas kernels for 17%

profile of v1, /device:TPU:0, one launch (start us, length us, event | category | flops | bytes accessed | tf_op | source)
XLA Modules:
  0.0 39.0 jit_solution(6001428585408584589)
XLA Ops:
  0.7 0.7 %copy.21 = f32[1,3,256]{2,1,0:T(4,128)S(1)} copy(f32[1,3,256]{2,0,1:T(1,128)} %param.11) | data formatting | bytes 6144
  1.4 0.3 copy-done
  1.8 0.7 %fusion.3 = (f32[1,256]{1,0:T(1,128)S(1)}, s32[1,256]{1,0:T(1,128)S(1)}) fusion(s32[1,1024]{1,0:T(1,128)} %param.10, s32[]{:T(128)S(6)} %select_n.50), kind=kLoop, calls=%fused_computation.26 | loop fusion | flops 256 | bytes 3076 | tf_op jit(solution)/shard_map/convert_element_type | solution.py:420
  2.5 4.0 %collective-permute-start = (f32[36,640]{1,0:T(8,128)S(1)}, f32[36,640]{1,0:T(8,128)S(1)}, u32[]{:S(2)}, u32[]{:S(2)}) collective-permute-start(f32[36,640]{1,0:T(8,128)S(1)} %pad_maximum_fusion), channel_id=1, source_target_pairs={{0,9},{1,8},{2,11},{3,10},{4,13},{5,12},{6,15},{7,14},{8,1},{9,0},... | collective-permute-start | bytes 276488 | tf_op jit(solution)/shard_map/ppermute | solution.py:427
  6.5 1.0 %copy.13 = bf16[32,32,8]{0,1,2:T(8,128)(2,1)S(1)} copy(bf16[32,32,8]{1,2,0:T(8,128)(2,1)} %param.7) | data formatting | bytes 32768 | tf_op args[1]
  7.5 0.7 %copy-done.1 = f32[32,27]{1,0:T(8,128)S(1)} copy-done((f32[32,27]{1,0:T(8,128)S(1)}, f32[32,27]{1,0:T(8,128)}, u32[]{:S(2)}) %copy-start.1) | copy-done | bytes 3480
  8.2 0.5 %shard_map.77.wide_ref = bf16[4,128,256]{2,1,0:T(8,128)(2,1)S(1)} custom-call(f32[8,32,32]{2,1,0:T(8,128)S(1)} %convert_bitcast_fusion.taps_ref, f32[32,27]{1,0:T(8,128)S(1)} %copy-done.1), custom_call_target="tpu_custom_call" | custom-call | tf_op jit(solution)/shard_map/pallas_call | solution.py:392
  8.8 0.6 %shard_map.78.refs_8_ = bf16[2,192,256]{2,1,0:T(8,128)(2,1)S(1)} custom-call(f32[8,32,32]{2,1,0:T(8,128)S(1)} %convert_bitcast_fusion.taps_ref, f32[32,27]{1,0:T(8,128)S(1)} %copy-done.1), custom_call_target="tpu_custom_call" | custom-call | tf_op jit(solution)/shard_map/pallas_call | solution.py:392
  9.4 4.7 %collective-permute-start.1 = (f32[40,640]{1,0:T(8,128)S(1)}, f32[40,640]{1,0:T(8,128)S(1)}, u32[]{:S(2)}, u32[]{:S(2)}) collective-permute-start(f32[40,640]{1,0:T(8,128)S(1)} %pad_maximum_fusion.1), channel_id=1, source_target_pairs={{0,19},{1,18},{2,17},{3,16},{4,23},{5,22},{6,21},{7,20},{8,27},{9,... | collective-permute-start | bytes 307208 | tf_op jit(solution)/shard_map/ppermute | solution.py:427
  14.2 0.8 %broadcast_multiply_fusion = bf16[4,8,4,2,32]{4,3,2,1,0:T(2,128)(2,1)S(1)} fusion(bf16[8,4,2]{2,1,0:T(4,128)(2,1)S(1)} %fusion.2, bf16[4,32]{1,0:T(4,128)(2,1)} %param.9), kind=kLoop, calls=%fused_computation.9 | loop fusion | flops 8192 | bytes 16768 | tf_op jit(solution)/shard_map/mul | solution.py:431
  15.1 4.0 %shard_map.79 = (f32[7,256,640]{2,1,0:T(8,128)}, f32[7,32,640]{2,1,0:T(8,128)S(1)}, bf16[2,288,640]{2,1,0:T(8,128)(2,1)S(1)}) custom-call(bf16[8,32,640]{2,1,0:T(8,128)(2,1)S(1)} %bitcast.22, bf16[4,128,256]{2,1,0:T(8,128)(2,1)S(1)} %shard_map.77.wide_ref, bf16[32,256]{1,0:T(8,128)(2,1)S(1)} %mul.34.point_ref), custom_call_target="tpu_custom_call" | custom-call | tf_op jit(solution)/shard_map/pallas_call | solution.py:392
  19.4 1.7 %shard_map.80 = (f32[2,256,640]{2,1,0:T(8,128)S(1)}, f32[2,32,640]{2,1,0:T(8,128)S(1)}, f32[16,640]{1,0:T(8,128)S(1)}) custom-call(s32[4]{0:T(128)S(1)} %pad_add_fusion.1.where_ref, f32[36,640]{1,0:T(8,128)S(1)} %collective-permute-done.one_ref, f32[40,640]{1,0:T(8,128)S(1)} %collective-permute-done.1.two_ref, ...), custom_call_target="tpu_custom_call" | custom-call | tf_op jit(solution)/shard_map/pallas_call | solution.py:392
  21.0 1.6 %shard_map.81.refs_0_ = f32[32,640]{1,0:T(8,128)S(1)} custom-call(s32[4]{0:T(128)S(1)} %pad_add_fusion.1.where_ref, f32[16,640]{1,0:T(8,128)S(1)} %get-tuple-element.23.tot_ref, f32[16,256]{1,0:T(8,128)S(1)} %pad_maximum_fusion.2.own_ref, f32[16,256]{1,0:T(8,128)S(1)} %collective-permute-done.2.other_ref), custom_call_target="tpu_custom_call" | custom-call | tf_op jit(solution)/shard_map/pallas_call | solution.py:392
  22.7 0.6 %collective-permute-start.3 = (f32[32,640]{1,0:T(8,128)S(1)}, f32[32,640]{1,0:T(8,128)S(1)}, u32[]{:S(2)}, u32[]{:S(2)}) collective-permute-start(f32[32,640]{1,0:T(8,128)S(1)} %shard_map.81.refs_0_), channel_id=1, source_target_pairs={{0,1},{1,2},{2,3},{3,0},{4,5},{5,6},{6,7},{7,4},{8,9},{9,10},{10,1... | collective-permute-start | bytes 245768 | tf_op jit(solution)/shard_map/ppermute | solution.py:498
  23.2 0.7 %collective-permute-start.4 = (f32[32,640]{1,0:T(8,128)S(1)}, f32[32,640]{1,0:T(8,128)S(1)}, u32[]{:S(2)}, u32[]{:S(2)}) collective-permute-start(f32[32,640]{1,0:T(8,128)S(1)} %shard_map.81.refs_0_), channel_id=1, source_target_pairs={{0,2},{1,3},{2,0},{3,1},{4,6},{5,7},{6,4},{7,5},{8,10},{9,11},{10,... | collective-permute-start | bytes 245768 | tf_op jit(solution)/shard_map/ppermute | solution.py:498
  24.0 2.8 %collective-permute-start.5 = (f32[32,640]{1,0:T(8,128)S(1)}, f32[32,640]{1,0:T(8,128)S(1)}, u32[]{:S(2)}, u32[]{:S(2)}) collective-permute-start(f32[32,640]{1,0:T(8,128)S(1)} %shard_map.81.refs_0_), channel_id=1, source_target_pairs={{0,3},{1,0},{2,1},{3,2},{4,7},{5,4},{6,5},{7,6},{8,11},{9,8},{10,9... | collective-permute-start | bytes 245768 | tf_op jit(solution)/shard_map/ppermute | solution.py:498
  26.8 2.1 %collective-permute-done.3.refs_1_ = f32[32,640]{1,0:T(8,128)S(1)} collective-permute-done((f32[32,640]{1,0:T(8,128)S(1)}, f32[32,640]{1,0:T(8,128)S(1)}, u32[]{:S(2)}, u32[]{:S(2)}) %collective-permute-start.3) | collective-permute-done | bytes 81952 | tf_op jit(solution)/shard_map/ppermute | solution.py:498
  28.9 0.7 %collective-permute-done.4.refs_2_ = f32[32,640]{1,0:T(8,128)S(1)} collective-permute-done((f32[32,640]{1,0:T(8,128)S(1)}, f32[32,640]{1,0:T(8,128)S(1)}, u32[]{:S(2)}, u32[]{:S(2)}) %collective-permute-start.4) | collective-permute-done | bytes 81952 | tf_op jit(solution)/shard_map/ppermute | solution.py:498
  29.6 0.4 %collective-permute-done.5.refs_3_ = f32[32,640]{1,0:T(8,128)S(1)} collective-permute-done((f32[32,640]{1,0:T(8,128)S(1)}, f32[32,640]{1,0:T(8,128)S(1)}, u32[]{:S(2)}, u32[]{:S(2)}) %collective-permute-start.5) | collective-permute-done | bytes 81952 | tf_op jit(solution)/shard_map/ppermute | solution.py:498
  30.0 5.3 %shard_map.82 = (f32[256,512]{1,0:T(8,128)S(1)}, f32[3,512]{1,0:T(4,128)S(1)}) custom-call(s32[4]{0:T(128)S(1)} %pad_add_fusion.1.where_ref, f32[32,640]{1,0:T(8,128)S(1)} %shard_map.81.refs_0_, f32[32,640]{1,0:T(8,128)S(1)} %collective-permute-done.3.refs_1_, f32[32,640]{1,0:T(8,128)S(1)} %collective-permute-done.4.refs_2_, ...), custom_call_target="tpu_custom_call" | custom-call | tf_op jit(solution)/shard_map/pallas_call | solution.py:392
  35.4 0.5 %collective-permute-start.6 = (f32[3,256]{1,0:T(4,128)S(1)}, f32[3,256]{1,0:T(4,128)S(1)}, u32[]{:S(2)}, u32[]{:S(2)}) collective-permute-start(f32[3,256]{1,0:T(4,128)S(1)} %slice.27), channel_id=1, source_target_pairs={{0,4},{4,0},{8,12},{12,8},{16,20},{20,16},{24,28},{28,24},{1,5},{5... | collective-permute-start | bytes 9224 | tf_op jit(solution)/shard_map/ppermute | solution.py:517
  35.9 1.4 %collective-permute-done.6 = f32[3,256]{1,0:T(4,128)S(1)} collective-permute-done((f32[3,256]{1,0:T(4,128)S(1)}, f32[3,256]{1,0:T(4,128)S(1)}, u32[]{:S(2)}, u32[]{:S(2)}) %collective-permute-start.6) | collective-permute-done | bytes 3104 | tf_op jit(solution)/shard_map/ppermute | solution.py:517
  37.3 0.6 %copy.15 = f32[1,3,256]{2,0,1:T(1,128)} copy(f32[1,3,256]{2,1,0:T(4,128)S(1)} %add_bitcast_fusion) | data formatting | bytes 6144
  37.9 1.2 %maximum_select_fusion = f32[32,8,1024]{2,1,0:T(8,128)} fusion(f32[32,8,512]{2,1,0:T(8,128)S(1)} %bitcast.25, f32[32,8,512]{2,1,0:T(8,128)S(1)} %bitcast.23, pred[]{:T(512)S(6)} %eq.19), kind=kLoop, calls=%fused_computation | loop fusion | flops 786432 | bytes 2097153 | tf_op jit(solution)/shard_map/jit(_where)/select_n | solution.py:518
  (29 shorter events, 0.7 us)
Async XLA Ops:
  0.6 1.1 %copy-start = (bf16[32,8,1024]{2,1,0:T(8,128)(2,1)S(1)}, bf16[32,8,1024]{2,1,0:T(8,128)(2,1)}, u32[]{:S(2)}) copy-start(bf16[32,8,1024]{2,1,0:T(8,128)(2,1)} %param.6) | copy-start | bytes 1572868
  2.5 6.9 %collective-permute-start = (f32[36,640]{1,0:T(8,128)S(1)}, f32[36,640]{1,0:T(8,128)S(1)}, u32[]{:S(2)}, u32[]{:S(2)}) collective-permute-start(f32[36,640]{1,0:T(8,128)S(1)} %pad_maximum_fusion), channel_id=1, source_target_pairs={{0,9},{1,8},{2,11},{3,10},{4,13},{5,12},{6,15},{7,14},{8,1},{9,0},... | collective-permute-start | bytes 276488 | tf_op jit(solution)/shard_map/ppermute | solution.py:427
  7.5 0.7 %copy-start.1 = (f32[32,27]{1,0:T(8,128)S(1)}, f32[32,27]{1,0:T(8,128)}, u32[]{:S(2)}) copy-start(f32[32,27]{1,0:T(8,128)} %depth_ref.3) | copy-start | bytes 10372
  9.4 9.6 %collective-permute-start.1 = (f32[40,640]{1,0:T(8,128)S(1)}, f32[40,640]{1,0:T(8,128)S(1)}, u32[]{:S(2)}, u32[]{:S(2)}) collective-permute-start(f32[40,640]{1,0:T(8,128)S(1)} %pad_maximum_fusion.1), channel_id=1, source_target_pairs={{0,19},{1,18},{2,17},{3,16},{4,23},{5,22},{6,21},{7,20},{8,27},{9,... | collective-permute-start | bytes 307208 | tf_op jit(solution)/shard_map/ppermute | solution.py:427
  19.1 1.9 %collective-permute-start.2 = (f32[16,256]{1,0:T(8,128)S(1)}, f32[16,256]{1,0:T(8,128)S(1)}, u32[]{:S(2)}, u32[]{:S(2)}) collective-permute-start(f32[16,256]{1,0:T(8,128)S(1)} %pad_maximum_fusion.2.own_ref), channel_id=1, source_target_pairs={{0,4},{4,0},{8,12},{12,8},{16,20},{20,16},{24,28},{28,24},{1,5},{5... | collective-permute-start | bytes 49160 | tf_op jit(solution)/shard_map/ppermute | solution.py:484
  22.7 6.2 %collective-permute-start.3 = (f32[32,640]{1,0:T(8,128)S(1)}, f32[32,640]{1,0:T(8,128)S(1)}, u32[]{:S(2)}, u32[]{:S(2)}) collective-permute-start(f32[32,640]{1,0:T(8,128)S(1)} %shard_map.81.refs_0_), channel_id=1, source_target_pairs={{0,1},{1,2},{2,3},{3,0},{4,5},{5,6},{6,7},{7,4},{8,9},{9,10},{10,1... | collective-permute-start | bytes 245768 | tf_op jit(solution)/shard_map/ppermute | solution.py:498
  23.2 6.3 %collective-permute-start.4 = (f32[32,640]{1,0:T(8,128)S(1)}, f32[32,640]{1,0:T(8,128)S(1)}, u32[]{:S(2)}, u32[]{:S(2)}) collective-permute-start(f32[32,640]{1,0:T(8,128)S(1)} %shard_map.81.refs_0_), channel_id=1, source_target_pairs={{0,2},{1,3},{2,0},{3,1},{4,6},{5,7},{6,4},{7,5},{8,10},{9,11},{10,... | collective-permute-start | bytes 245768 | tf_op jit(solution)/shard_map/ppermute | solution.py:498
  24.0 6.0 %collective-permute-start.5 = (f32[32,640]{1,0:T(8,128)S(1)}, f32[32,640]{1,0:T(8,128)S(1)}, u32[]{:S(2)}, u32[]{:S(2)}) collective-permute-start(f32[32,640]{1,0:T(8,128)S(1)} %shard_map.81.refs_0_), channel_id=1, source_target_pairs={{0,3},{1,0},{2,1},{3,2},{4,7},{5,4},{6,5},{7,6},{8,11},{9,8},{10,9... | collective-permute-start | bytes 245768 | tf_op jit(solution)/shard_map/ppermute | solution.py:498
  35.3 2.6 %collective-permute-start.7 = (f32[256,512]{1,0:T(8,128)S(1)}, f32[256,512]{1,0:T(8,128)S(1)}, u32[]{:S(2)}, u32[]{:S(2)}) collective-permute-start(f32[256,512]{1,0:T(8,128)S(1)} %get-tuple-element.29), channel_id=1, source_target_pairs={{0,4},{4,0},{8,12},{12,8},{16,20},{20,16},{24,28},{28,24},{1,5},{5... | collective-permute-start | bytes 1572872 | tf_op jit(solution)/shard_map/ppermute | solution.py:516
  35.4 1.9 %collective-permute-start.6 = (f32[3,256]{1,0:T(4,128)S(1)}, f32[3,256]{1,0:T(4,128)S(1)}, u32[]{:S(2)}, u32[]{:S(2)}) collective-permute-start(f32[3,256]{1,0:T(4,128)S(1)} %slice.27), channel_id=1, source_target_pairs={{0,4},{4,0},{8,12},{12,8},{16,20},{20,16},{24,28},{28,24},{1,5},{5... | collective-permute-start | bytes 9224 | tf_op jit(solution)/shard_map/ppermute | solution.py:517

commit v2 on v1

--- a/solution.py
+++ b/solution.py
@@ -66,14 +66,15 @@
         put(chans * (6 + j), pltpu.roll(by_y * keep(lane >= CY), width - CY, 1))
 
 
-def composed(taps_ref, weight, e):
+def composed(taps, depth, e):
     total = None
     for a in range(2):
         for b in range(2):
             for c in range(2):
                 d = (a + 2 - e[0], b + 2 - e[1], c + 2 - e[2])
                 if min(d) >= 0 and max(d) <= 2:
-                    term = weight(9 * d[0] + 3 * d[1] + d[2]) * taps_ref[4 * a + 2 * b + c]
+                    at = 9 * d[0] + 3 * d[1] + d[2]
+                    term = depth[at : at + 1, :] * taps[4 * a + 2 * b + c]
                     total = term if total is None else total + term
     return total
 
@@ -106,9 +107,15 @@
     raw_ref[k] = jnp.dot(point, jnp.concatenate(features, axis=0), preferred_element_type=F32)
 
 
-def weight_kernel(taps_ref, depth_ref, wide_ref, full_ref):
-    chans = taps_ref.shape[1]
-    columns = [jnp.broadcast_to(depth_ref[:, i : i + 1], (chans, chans)) for i in range(27)]
+def weight_kernel(
+    tconv_ref, depth_ref, weight_ref, wide_ref, turned_ref, point_ref, back_ref,
+    taps_ref, depth_pad_ref, full_ref, full2_ref,
+):
+    chans = tconv_ref.shape[0]
+    taps_ref[:, 0:chans] = tconv_ref[...].astype(F32).reshape(8 * chans, chans)
+    taps = [taps_ref[pl.ds(q, chans, stride=8), :][:, :chans] for q in range(8)]
+    depth_pad_ref[:, 0:27] = depth_ref[...]
+    depth = depth_pad_ref[...].T
     for b in range(2):
         for c in range(2):
             for first in range(2):
@@ -117,32 +124,55 @@
                         for ny in near(c):
                             e = (2 - 2 * j + first, b - 2 * nx + 1, c - 2 * ny + 1)
                             at = chans * (4 * j + 2 * (nx - near(b)[0]) + ny - near(c)[0])
-                            full_ref[2 * b + c, chans * first : chans * (first + 1), at : at + chans] = composed(
-                                taps_ref, lambda i: columns[i], e
-                            )
-    high = full_ref[...].astype(BF16)
-    wide_ref[:, : 2 * chans, :] = high
-    wide_ref[:, 2 * chans :, :] = (full_ref[...] - high.astype(F32)).astype(BF16)
-
-
-def turn_kernel(taps_ref, depth_ref, wide_ref, full_ref):
-    chans = taps_ref.shape[1]
-    full_ref[...] = jnp.zeros_like(full_ref)
-    columns = [jnp.broadcast_to(depth_ref[:, i : i + 1], (chans, chans)) for i in range(27)]
+                            col = chans * first
+                            full_ref[2 * b + c, at : at + chans, col : col + chans] = composed(taps, depth, e)
+            whole = full_ref[2 * b + c].T[: 2 * chans]
+            high = whole.astype(BF16)
+            wide_ref[2 * b + c, : 2 * chans, :] = high
+            wide_ref[2 * b + c, 2 * chans :, :] = (whole - high.astype(F32)).astype(BF16)
+    full2_ref[...] = jnp.zeros_like(full2_ref)
     for b in range(2):
         for n in range(2):
             nx = n - b
             for ny in (-1, 0, 1):
-                col = chans * (3 * n + ny + 1)
+                row = chans * (3 * n + ny + 1)
                 for j in range(4):
                     for c in range(2):
                         e = (j, 2 * nx + b + 1, 2 * ny + c + 1)
                         if 0 <= e[2] < 4:
-                            row = chans * (4 * (j // 2) + 2 * c + j % 2)
-                            full_ref[b, row : row + chans, col : col + chans] = composed(
-                                taps_ref, lambda i: columns[i], e
-                            )
-        wide_ref[b] = full_ref[b].T[: 6 * chans].astype(BF16)
+                            col = chans * (4 * (j // 2) + 2 * c + j % 2)
+                            full2_ref[b, row : row + chans, col : col + chans] = composed(taps, depth, e)
+    turned_ref[...] = full2_ref[...].astype(BF16)
+    weight = weight_ref[...].astype(F32)
+    lines = jnp.concatenate([weight] * 8, axis=1)
+    lines = jnp.concatenate([jnp.broadcast_to(lines[o : o + 1], (8, 8 * chans)) for o in range(4)], axis=0)
+    row = lax.broadcasted_iota(jnp.int32, lines.shape, 0) % 8
+    col = lax.broadcasted_iota(jnp.int32, lines.shape, 1) // chans
+    lines = jnp.where(col == 2 * (row % 4) + row // 4, lines, 0.0)
+    point_ref[...] = lines.astype(BF16)
+    turned = lines.T
+    back_ref[...] = jnp.concatenate([turned] * 3, axis=1).astype(BF16)
+
+
+def pack_kernel(where_ref, window_ref, targets_ref, ids_ref, one_ref, two_ref):
+    depth, chans, width = window_ref.shape
+    count = targets_ref.shape[2]
+    slab = where_ref[0]
+    even = lax.rem(slab, 2) == 0
+    first, last = window_ref[0].astype(F32), window_ref[depth - 1].astype(F32)
+    ids = ids_ref[:, pl.ds(pl.multiple_of(slab * count, 128), count)].astype(F32)
+    block = jnp.concatenate([targets_ref[0], targets_ref[1], targets_ref[2], ids], axis=0)
+    rows = jnp.concatenate([thirds(block).astype(F32), jnp.zeros((4, count), F32)], axis=0)
+    rows = jnp.concatenate([rows, jnp.zeros((16, width - count), F32)], axis=1).astype(BF16)
+    one_ref[0:chans, :] = jnp.where(even, last, first).astype(BF16)
+    two_ref[0:chans, :] = jnp.where(even, first, last).astype(BF16)
+    one_ref[chans : chans + 16, :] = rows
+    two_ref[chans : chans + 16, :] = rows
+
+
+def block_at(ref, j, count):
+    x = ref[:, count * j : count * (j + 1)].astype(F32)
+    return x[0:4] + x[4:8] + x[8:12]
 
 
 def inner_kernel(lat_ref, wide_ref, point_ref, away_ref, raw_ref, edge_ref, x9_ref, slope_ref, sems):
@@ -176,7 +206,7 @@
     chans = edge_ref.shape[1] // 9
     pairs = inner_ref.shape[0] + 2
     even = lax.rem(slab, 2) == 0
-    one, two = one_ref[0:chans, :], two_ref[0:chans, :]
+    one, two = one_ref[0:chans, :].astype(F32), two_ref[0:chans, :].astype(F32)
     low = jnp.where(slab == 0, 0.0, jnp.where(even, two, one))
     high = jnp.where(slab == slabs - 1, 0.0, jnp.where(even, one, two))
     for k, x in ((0, low), (1, high)):
@@ -221,17 +251,19 @@
     return (fine_x // 2) * CY + fine_y // 2, (fine_x % 2) * 2 + fine_y % 2
 
 
-def target_kernel(where_ref, tot_ref, own_ref, other_ref, msg_ref):
+def target_kernel(count, where_ref, tot_ref, *refs):
+    *block_refs, msg_ref, near_ref = refs
     width = tot_ref.shape[1]
     start = where_ref[1]
     msg_ref[0:16, :] = tot_ref[...]
-    count = own_ref.shape[1]
     row = lax.broadcasted_iota(jnp.int32, (16, count), 0)
     cells = lax.broadcasted_iota(jnp.int32, (count, width), 1)
     total = jnp.zeros((48, width), F32)
-    for ref in (own_ref, other_ref):
-        for j in range(ref.shape[0] // 4):
-            block = ref[4 * j : 4 * j + 4, :]
+    for i, ref in enumerate(block_refs):
+        for j in range(ref.shape[1] // count):
+            block = block_at(ref, j, count)
+            if j == 0:
+                near_ref[:, count * i : count * (i + 1)] = block[3:4, :].astype(jnp.int32)
             cell, part = cell_of(block[3:4, :].astype(jnp.int32))
             value = jnp.where(row < 4, 1.0, jnp.where(row < 8, block[0:1, :], jnp.where(row < 12, block[1:2, :], block[2:3, :])))
             value = jnp.where(row % 4 == part, value, 0.0)
@@ -251,8 +283,9 @@
     chans = slope_ref.shape[1] // 8
     own_width = grad_ref.shape[1]
     second = lax.broadcasted_iota(jnp.int32, (8, width), 0) >= 4
-    for k in range(inner):
-        pltpu.make_async_copy(away_ref.at[k], slope_ref.at[k], sems.at[k]).start()
+    loads = [pltpu.make_async_copy(away_ref.at[k], slope_ref.at[k], sems.at[k]) for k in range(inner)]
+    for load in loads:
+        load.start()
 
     def both(x):
         other = swap(x)
@@ -344,10 +377,8 @@
 
     def pair(k):
         if 0 < k < last:
-            pltpu.make_async_copy(away_ref.at[k - 1], slope_ref.at[k - 1], sems.at[k - 1]).wait()
-            slope = slope_ref[k - 1]
-        else:
-            slope = slope2_ref[k // last]
+            loads[k - 1].wait()
+        slope = slope_ref[k - 1] if 0 < k < last else slope2_ref[k // last]
         grad_features = jnp.dot(point_ref[...], thirds(e_ref[k]), preferred_element_type=F32)
         gdw_ref[k] = (grad_features * slope).astype(BF16)
 
@@ -378,14 +409,15 @@
         grad_ref[:, 128 * t : 128 * t + 128] = tile_ref[t]
 
 
-def call(kernel, outs, scratch, operands, smem, away_in=None, away_out=None):
+def call(kernel, outs, scratch, operands, smem, far=(), away=(), away_out=None):
     operands = list(operands)
     specs = [SM] * smem + [VM] * (len(operands) - smem)
     out_specs = [VM] * len(outs)
     shapes = [jax.ShapeDtypeStruct(s, t) for s, t in outs]
-    if away_in is not None:
-        operands[away_in] = pltpu.with_memory_space_constraint(operands[away_in], pltpu.HBM)
-        specs[away_in] = pl.BlockSpec(memory_space=pltpu.HBM)
+    for i in far:
+        operands[i] = pltpu.with_memory_space_constraint(operands[i], pltpu.HBM)
+    for i in away:
+        specs[i] = pl.BlockSpec(memory_space=pltpu.HBM)
     if away_out is not None:
         shapes[away_out] = pltpu.HBM(*outs[away_out])
         out_specs[away_out] = pl.BlockSpec(memory_space=pltpu.HBM)
@@ -414,52 +446,41 @@
     scale = 1.5 / (2 * depth * slabs)
 
     window = lax.dynamic_slice_in_dim(jnp.transpose(latent, (1, 0, 2)), start, width, axis=2)
-    even = slab % 2 == 0
-    first, last = window[0].astype(F32), window[depth - 1].astype(F32)
-    ids = lax.dynamic_slice_in_dim(pencil_ids, slab * count, count, axis=1)
-    blocks = jnp.concatenate([targets[0], ids.astype(F32)], axis=0)
-
-    def widened(x):
-        return jnp.pad(x, ((0, 0), (0, width - count)))
+    one, two = call(
+        pack_kernel,
+        [((chans + 16, width), BF16)] * 2,
+        [],
+        (where, window, jnp.transpose(targets, (1, 0, 2)), pencil_ids),
+        1,
+        far=(2, 3),
+    )
 
     def send(x, mask, partner):
         pairs = [(v * slabs + s, (v ^ mask) * slabs + partner(s)) for v in range(views) for s in range(slabs)]
         return lax.ppermute(x, ("view", "slab"), pairs)
 
-    taps = jnp.transpose(tconv_weight.astype(F32), (2, 1, 0))
-    eye = jnp.eye(8, dtype=BF16)
-    point = point_weight[:, None, None, :] * eye[None, :, :, None]
-    point = jnp.transpose(point.reshape(4, 8, 2, 4, chans), (0, 1, 3, 2, 4)).reshape(32, 8 * chans)
-    point_back = jnp.tile(point.T, (1, 3))
-    (wide,) = call(
+    wide, turned, point, point_back = call(
         weight_kernel,
-        [((4, 4 * chans, 8 * chans), BF16)],
-        [((4, 2 * chans, 8 * chans), F32)],
-        (taps, depth_weight),
+        [
+            ((4, 4 * chans, 8 * chans), BF16),
+            ((2, 6 * chans, 8 * chans), BF16),
+            ((32, 8 * chans), BF16),
+            ((8 * chans, 96), BF16),
+        ],
+        [((8 * chans, 128), F32), ((chans, 128), F32), ((4, 8 * chans, 128), F32), ((2, 6 * chans, 8 * chans), F32)],
+        (jnp.transpose(tconv_weight, (0, 2, 1)), depth_weight, point_weight),
         0,
-    )
-    (turned,) = call(
-        turn_kernel,
-        [((2, 6 * chans, 8 * chans), BF16)],
-        [((2, 8 * chans, 8 * chans), F32)],
-        (taps, depth_weight),
-        0,
+        far=(0, 1, 2),
     )
 
     masks = [split << k for k in range((views // split).bit_length() - 1)]
-    one = send(
-        jnp.concatenate([jnp.where(even, last, first), widened(blocks)], axis=0),
-        masks[0] if masks else 0,
-        lambda s: (s + 1 - 2 * (s % 2)) % slabs,
-    )
-    one, wide, turned = lax.optimization_barrier((one, wide, turned))
+    blocks = two[chans:, :count]
+    one = send(one, masks[0] if masks else 0, lambda s: (s + 1 - 2 * (s % 2)) % slabs)
+    one, wide = lax.optimization_barrier((one, wide))
     if masks:
-        blocks = jnp.concatenate([blocks, one[chans:, :count]], axis=0)
-    two = send(
-        jnp.concatenate([jnp.where(even, first, last), widened(blocks)], axis=0),
-        masks[1] if len(masks) > 1 else 0,
-        lambda s: (s + 2 * (s % 2) - 1) % slabs,
-    )
+        two = lax.dynamic_update_slice(two, one[chans:, :count], (chans, count))
+        blocks = two[chans:, : 2 * count]
+    two = send(two, masks[1] if len(masks) > 1 else 0, lambda s: (s + 2 * (s % 2) - 1) % slabs)
     inner = depth - 1
     slope, raw, edge = call(
         inner_kernel,
@@ -475,16 +496,13 @@
     )
     two, raw, edge = lax.optimization_barrier((two, raw, edge))
     if len(masks) > 1:
-        blocks = jnp.concatenate([blocks, two[chans:, :count]], axis=0)
+        blocks = jnp.concatenate([blocks, two[chans:, : 2 * count]], axis=1)
     for mask in masks[2:]:
-        blocks = jnp.concatenate([blocks, send(blocks, mask, lambda s: s)], axis=0)
-    own_blocks = blocks
+        blocks = jnp.concatenate([blocks, send(blocks, mask, lambda s: s)], axis=1)
+    groups = [blocks]
     if split == 2:
         pairing = [(i, i ^ 1) for i in range(views)]
-        other_blocks = lax.ppermute(own_blocks, "view", pairing)
-        near_ids = jnp.concatenate([ids, other_blocks[3:4].astype(jnp.int32)], axis=1)
-    else:
-        other_blocks, near_ids = own_blocks[:0], ids
+        groups.append(lax.ppermute(blocks, "view", pairing))
     slope2, raw2, tot = call(
         functools.partial(outer_kernel, scale),
         [((2, 8 * chans, width), F32), ((2, 32, width), F32), ((16, width), F32)],
@@ -492,7 +510,13 @@
         (where, one, two, edge, wide, point, raw),
         1,
     )
-    (message,) = call(target_kernel, [((32, width), F32)], [], (where, tot, own_blocks, other_blocks), 1)
+    message, near_ids = call(
+        functools.partial(target_kernel, count),
+        [((32, width), F32), ((1, split * count), jnp.int32)],
+        [],
+        (where, tot, *groups),
+        1,
+    )
     messages = [message]
     for k in range(1, slabs):
         messages.append(lax.ppermute(message, "slab", [(i, (i + k) % slabs) for i in range(slabs)]))
@@ -509,7 +533,8 @@
         ],
         (where, *messages, raw, raw2, slope, slope2, turned, point_back, near_ids),
         1,
-        away_in=slabs + 3,
+        far=(slabs + 3,),
+        away=(slabs + 3,),
     )
     colour = found[:, :count]
     if split == 2:

time: 39.4 us -> 37.4 us (0.949)
  local copies, waits for them, and re-layouts: 3.59 us -> 1.69 us
  other arithmetic: 2.82 us -> 1.24 us
  Pallas kernels: 13.7 us -> 15.2 us
  waiting for transfers between devices: 4.63 us -> 5.28 us
  starting transfers between devices: 13.5 us -> 13 us
    unnamed x8 -> x4, local copies, waits for them, and re-layouts: 3.32 us -> 1.64 us
    pallas_call x6, Pallas kernels: 13.7 us -> 15.2 us  [call(): pl.pallas_call(kernel, out_shape=shapes, in_specs=specs, out_specs=out_sp...]
    mul x1 -> x0, other arithmetic: 0.8 us -> none  [on_device(): point = point_weight[:, None, None, :] * eye[None, :, :, None]]
    convert_element_type x3 -> x0, other arithmetic: 0.7 us -> none  [the longest x1 0.69 us: on_device(): blocks = jnp.concatenate([targets[0], ids.astype(F32)], axis=0)]
    ppermute x3, starting transfers between devices: 4.14 us -> 3.48 us  [on_device(): lax.ppermute(message, 'slab', [(i, (i + k) % slabs) for i in range(slabs)])]
  transfers between devices with their start and end apart: 8 -> 8, of which waited for: 5 -> 4; matrix products, arithmetic and copies ran while one was open for 7% -> 2% of each run, Pallas kernels for 17% -> 20%
where the time goes in v2:
time: 37.4 us; the launch traced here: 37.2 us
  Pallas kernels  15.2 us (41%)
  starting transfers between devices  13 us (35%)
  waiting for transfers between devices  5.28 us (14%)
  local copies, waits for them, and re-layouts  1.69 us (5%)
  other arithmetic  1.24 us (3%)
  between operations  0.78 us (2%)
    pallas_call x6, Pallas kernels, call(): pl.pallas_call(kernel, out_shape=shapes, in_specs=specs, out_specs=out_sp...  15.2 us
    ppermute x2, starting transfers between devices, send(): return lax.ppermute(x, ('view', 'slab'), pairs)  8.9 us
    ppermute x3, starting transfers between devices, on_device(): lax.ppermute(message, 'slab', [(i, (i + k) % slabs) for i in range(slabs)])  3.48 us
    ppermute x3, waiting for transfers between devices, on_device(): lax.ppermute(message, 'slab', [(i, (i + k) % slabs) for i in range(slabs)])  3.42 us
    unnamed x4, local copies, waits for them, and re-layouts  1.64 us
    ppermute x1, waiting for transfers between devices, on_device(): colour = colour + lax.ppermute(found[:, count:], 'view', pairing)  1.4 us
    select_n x1, other arithmetic, on_device(): jnp.where(half == 0, jnp.concatenate([grad, other], axis=1), jnp.concaten...  1.15 us
  transfers between devices with their start and end apart: 8, of which 4 were waited for; matrix products, arithmetic and copies ran while one was open for 2% of the time, Pallas kernels for 20%

profile of v2, /device:TPU:0, one launch (start us, length us, event | category | flops | bytes accessed | tf_op | source)
XLA Modules:
  0.0 37.2 jit_solution(15871353430841949572)
XLA Ops:
  0.6 0.0 copy-start
  0.7 1.0 %copy-done = bf16[32,8,1024]{2,1,0:T(8,128)(2,1)S(1)} copy-done((bf16[32,8,1024]{2,1,0:T(8,128)(2,1)S(1)}, bf16[32,8,1024]{2,1,0:T(8,128)(2,1)}, u32[]{:S(2)}) %copy-start) | copy-done | bytes 524312
  1.8 0.1 pad_add_fusion.where_ref
  1.8 0.7 %shard_map.77 = (bf16[48,640]{1,0:T(8,128)(2,1)S(1)}, bf16[48,640]{1,0:T(8,128)(2,1)S(1)}) custom-call(s32[4]{0:T(128)S(1)} %pad_add_fusion.where_ref, bf16[8,32,640]{2,1,0:T(8,128)(2,1)S(1)} %bitcast.12, f32[3,1,256]{2,1,0:T(1,128)} %bitcast.17, s32[1,1024]{1,0:T(1,128)} %ids_ref.1), custom_call_target="tpu_custom_call" | custom-call | tf_op jit(solution)/shard_map/pallas_call | solution.py:424
  2.6 4.0 %collective-permute-start = (bf16[48,640]{1,0:T(8,128)(2,1)S(1)}, bf16[48,640]{1,0:T(8,128)(2,1)S(1)}, u32[]{:S(2)}, u32[]{:S(2)}) collective-permute-start(bf16[48,640]{1,0:T(8,128)(2,1)S(1)} %get-tuple-element.23), channel_id=1, source_target_pairs={{0,9},{1,8},{2,11},{3,10},{4,13},{5,12},{6,15},{7,14},{8,1},{9,0},... | collective-permute-start | bytes 184328 | tf_op jit(solution)/shard_map/ppermute | solution.py:460
  6.6 1.7 %shard_map.78 = (bf16[4,128,256]{2,1,0:T(8,128)(2,1)S(1)}, bf16[2,192,256]{2,1,0:T(8,128)(2,1)S(1)}, bf16[32,256]{1,0:T(8,128)(2,1)S(1)}, bf16[256,96]{1,0:T(8,128)(2,1)S(1)}) custom-call(bf16[32,8,32]{2,1,0:T(8,128)(2,1)} %bitcast.16, f32[32,27]{1,0:T(8,128)} %depth_ref.1, bf16[4,32]{1,0:T(4,128)(2,1)} %weight_ref.1), custom_call_target="tpu_custom_call" | custom-call | tf_op jit(solution)/shard_map/pallas_call | solution.py:424
  8.4 0.4 %collective-permute-done.one_ref = bf16[48,640]{1,0:T(8,128)(2,1)S(1)} collective-permute-done((bf16[48,640]{1,0:T(8,128)(2,1)S(1)}, bf16[48,640]{1,0:T(8,128)(2,1)S(1)}, u32[]{:S(2)}, u32[]{:S(2)}) %collective-permute-start) | collective-permute-done | bytes 61472 | tf_op jit(solution)/shard_map/ppermute | solution.py:460
  8.8 4.9 %collective-permute-start.1 = (bf16[48,640]{1,0:T(8,128)(2,1)S(1)}, bf16[48,640]{1,0:T(8,128)(2,1)S(1)}, u32[]{:S(2)}, u32[]{:S(2)}) collective-permute-start(bf16[48,640]{1,0:T(8,128)(2,1)S(1)} %slice_dynamic-update-slice_fusion), channel_id=1, source_target_pairs={{0,19},{1,18},{2,17},{3,16},{4,23},{5,22},{6,21},{7,20},{8,27},{9,... | collective-permute-start | bytes 184328 | tf_op jit(solution)/shard_map/ppermute | solution.py:460
  13.7 4.0 %shard_map.79 = (f32[7,256,640]{2,1,0:T(8,128)}, f32[7,32,640]{2,1,0:T(8,128)S(1)}, bf16[2,288,640]{2,1,0:T(8,128)(2,1)S(1)}) custom-call(bf16[8,32,640]{2,1,0:T(8,128)(2,1)S(1)} %bitcast.13, bf16[4,128,256]{2,1,0:T(8,128)(2,1)S(1)} %get-tuple-element.27.wide_ref, bf16[32,256]{1,0:T(8,128)(2,1)S(1)} %get-tuple-element.28.point_ref), custom_call_target="tpu_custom_call" | custom-call | tf_op jit(solution)/shard_map/pallas_call | solution.py:424
  17.7 0.0 collective-permute-done.1.two_ref
  17.7 0.1 collective-permute-start.2
  17.8 1.7 %shard_map.80 = (f32[2,256,640]{2,1,0:T(8,128)S(1)}, f32[2,32,640]{2,1,0:T(8,128)S(1)}, f32[16,640]{1,0:T(8,128)S(1)}) custom-call(s32[4]{0:T(128)S(1)} %pad_add_fusion.where_ref, bf16[48,640]{1,0:T(8,128)(2,1)S(1)} %collective-permute-done.one_ref, bf16[48,640]{1,0:T(8,128)(2,1)S(1)} %collective-permute-done.1.two_ref, ...), custom_call_target="tpu_custom_call" | custom-call | tf_op jit(solution)/shard_map/pallas_call | solution.py:424
  19.5 1.6 %shard_map.81 = (f32[32,640]{1,0:T(8,128)S(1)}, s32[1,512]{1,0:T(1,128)S(1)}) custom-call(s32[4]{0:T(128)S(1)} %pad_add_fusion.where_ref, f32[16,640]{1,0:T(8,128)S(1)} %get-tuple-element.34.tot_ref, bf16[16,1024]{1,0:T(8,128)(2,1)S(1)} %pad_maximum_fusion.refs_0_, bf16[16,1024]{1,0:T(8,128)(2,1)S(1)} %collective-permute-done.2.refs_1_), custom_call_target="tpu_custom_call" | custom-call | tf_op jit(solution)/shard_map/pallas_call | solution.py:424
  21.1 0.6 %collective-permute-start.3 = (f32[32,640]{1,0:T(8,128)S(1)}, f32[32,640]{1,0:T(8,128)S(1)}, u32[]{:S(2)}, u32[]{:S(2)}) collective-permute-start(f32[32,640]{1,0:T(8,128)S(1)} %get-tuple-element.35.refs_0_), channel_id=1, source_target_pairs={{0,1},{1,2},{2,3},{3,0},{4,5},{5,6},{6,7},{7,4},{8,9},{9,10},{10,1... | collective-permute-start | bytes 245768 | tf_op jit(solution)/shard_map/ppermute | solution.py:522
  21.7 0.9 %collective-permute-start.4 = (f32[32,640]{1,0:T(8,128)S(1)}, f32[32,640]{1,0:T(8,128)S(1)}, u32[]{:S(2)}, u32[]{:S(2)}) collective-permute-start(f32[32,640]{1,0:T(8,128)S(1)} %get-tuple-element.35.refs_0_), channel_id=1, source_target_pairs={{0,2},{1,3},{2,0},{3,1},{4,6},{5,7},{6,4},{7,5},{8,10},{9,11},{10,... | collective-permute-start | bytes 245768 | tf_op jit(solution)/shard_map/ppermute | solution.py:522
  22.6 2.0 %collective-permute-start.5 = (f32[32,640]{1,0:T(8,128)S(1)}, f32[32,640]{1,0:T(8,128)S(1)}, u32[]{:S(2)}, u32[]{:S(2)}) collective-permute-start(f32[32,640]{1,0:T(8,128)S(1)} %get-tuple-element.35.refs_0_), channel_id=1, source_target_pairs={{0,3},{1,0},{2,1},{3,2},{4,7},{5,4},{6,5},{7,6},{8,11},{9,8},{10,9... | collective-permute-start | bytes 245768 | tf_op jit(solution)/shard_map/ppermute | solution.py:522
  24.6 2.8 %collective-permute-done.3.refs_1_ = f32[32,640]{1,0:T(8,128)S(1)} collective-permute-done((f32[32,640]{1,0:T(8,128)S(1)}, f32[32,640]{1,0:T(8,128)S(1)}, u32[]{:S(2)}, u32[]{:S(2)}) %collective-permute-start.3) | collective-permute-done | bytes 81952 | tf_op jit(solution)/shard_map/ppermute | solution.py:522
  27.4 0.7 %collective-permute-done.4.refs_2_ = f32[32,640]{1,0:T(8,128)S(1)} collective-permute-done((f32[32,640]{1,0:T(8,128)S(1)}, f32[32,640]{1,0:T(8,128)S(1)}, u32[]{:S(2)}, u32[]{:S(2)}) %collective-permute-start.4) | collective-permute-done | bytes 81952 | tf_op jit(solution)/shard_map/ppermute | solution.py:522
  28.0 5.4 %shard_map.82 = (f32[256,512]{1,0:T(8,128)S(1)}, f32[3,512]{1,0:T(4,128)S(1)}) custom-call(s32[4]{0:T(128)S(1)} %pad_add_fusion.where_ref, f32[32,640]{1,0:T(8,128)S(1)} %get-tuple-element.35.refs_0_, f32[32,640]{1,0:T(8,128)S(1)} %collective-permute-done.3.refs_1_, f32[32,640]{1,0:T(8,128)S(1)} %collective-permute-done.4.refs_2_, ...), custom_call_target="tpu_custom_call" | custom-call | tf_op jit(solution)/shard_map/pallas_call | solution.py:424
  33.4 0.1 collective-permute-start.7
  33.5 0.5 %collective-permute-start.6 = (f32[3,256]{1,0:T(4,128)S(1)}, f32[3,256]{1,0:T(4,128)S(1)}, u32[]{:S(2)}, u32[]{:S(2)}) collective-permute-start(f32[3,256]{1,0:T(4,128)S(1)} %slice.19), channel_id=1, source_target_pairs={{0,4},{4,0},{8,12},{12,8},{16,20},{20,16},{24,28},{28,24},{1,5},{5... | collective-permute-start | bytes 9224 | tf_op jit(solution)/shard_map/ppermute | solution.py:542
  34.0 1.4 %collective-permute-done.6 = f32[3,256]{1,0:T(4,128)S(1)} collective-permute-done((f32[3,256]{1,0:T(4,128)S(1)}, f32[3,256]{1,0:T(4,128)S(1)}, u32[]{:S(2)}, u32[]{:S(2)}) %collective-permute-start.6) | collective-permute-done | bytes 3104 | tf_op jit(solution)/shard_map/ppermute | solution.py:542
  35.4 0.6 %copy.9 = f32[1,3,256]{2,0,1:T(1,128)} copy(f32[1,3,256]{2,1,0:T(4,128)S(1)} %add_bitcast_fusion) | data formatting | bytes 6144
  36.0 1.1 %maximum_select_fusion = f32[32,8,1024]{2,1,0:T(8,128)} fusion(f32[32,8,512]{2,1,0:T(8,128)S(1)} %bitcast.15, f32[32,8,512]{2,1,0:T(8,128)S(1)} %bitcast.14, pred[]{:T(512)S(6)} %eq.5), kind=kLoop, calls=%fused_computation | loop fusion | flops 786432 | bytes 2097153 | tf_op jit(solution)/shard_map/jit(_where)/select_n | solution.py:543
  (11 shorter events, 0.1 us)
Async XLA Ops:
  0.6 1.0 %copy-start = (bf16[32,8,1024]{2,1,0:T(8,128)(2,1)S(1)}, bf16[32,8,1024]{2,1,0:T(8,128)(2,1)}, u32[]{:S(2)}) copy-start(bf16[32,8,1024]{2,1,0:T(8,128)(2,1)} %param.6) | copy-start | bytes 1572868
  2.6 6.2 %collective-permute-start = (bf16[48,640]{1,0:T(8,128)(2,1)S(1)}, bf16[48,640]{1,0:T(8,128)(2,1)S(1)}, u32[]{:S(2)}, u32[]{:S(2)}) collective-permute-start(bf16[48,640]{1,0:T(8,128)(2,1)S(1)} %get-tuple-element.23), channel_id=1, source_target_pairs={{0,9},{1,8},{2,11},{3,10},{4,13},{5,12},{6,15},{7,14},{8,1},{9,0},... | collective-permute-start | bytes 184328 | tf_op jit(solution)/shard_map/ppermute | solution.py:460
  8.8 8.9 %collective-permute-start.1 = (bf16[48,640]{1,0:T(8,128)(2,1)S(1)}, bf16[48,640]{1,0:T(8,128)(2,1)S(1)}, u32[]{:S(2)}, u32[]{:S(2)}) collective-permute-start(bf16[48,640]{1,0:T(8,128)(2,1)S(1)} %slice_dynamic-update-slice_fusion), channel_id=1, source_target_pairs={{0,19},{1,18},{2,17},{3,16},{4,23},{5,22},{6,21},{7,20},{8,27},{9,... | collective-permute-start | bytes 184328 | tf_op jit(solution)/shard_map/ppermute | solution.py:460
  17.7 1.8 %collective-permute-start.2 = (bf16[16,1024]{1,0:T(8,128)(2,1)S(1)}, bf16[16,1024]{1,0:T(8,128)(2,1)S(1)}, u32[]{:S(2)}, u32[]{:S(2)}) collective-permute-start(bf16[16,1024]{1,0:T(8,128)(2,1)S(1)} %pad_maximum_fusion.refs_0_), channel_id=1, source_target_pairs={{0,4},{4,0},{8,12},{12,8},{16,20},{20,16},{24,28},{28,24},{1,5},{5... | collective-permute-start | bytes 98312 | tf_op jit(solution)/shard_map/ppermute | solution.py:505
  21.1 6.2 %collective-permute-start.3 = (f32[32,640]{1,0:T(8,128)S(1)}, f32[32,640]{1,0:T(8,128)S(1)}, u32[]{:S(2)}, u32[]{:S(2)}) collective-permute-start(f32[32,640]{1,0:T(8,128)S(1)} %get-tuple-element.35.refs_0_), channel_id=1, source_target_pairs={{0,1},{1,2},{2,3},{3,0},{4,5},{5,6},{6,7},{7,4},{8,9},{9,10},{10,1... | collective-permute-start | bytes 245768 | tf_op jit(solution)/shard_map/ppermute | solution.py:522
  21.7 6.3 %collective-permute-start.4 = (f32[32,640]{1,0:T(8,128)S(1)}, f32[32,640]{1,0:T(8,128)S(1)}, u32[]{:S(2)}, u32[]{:S(2)}) collective-permute-start(f32[32,640]{1,0:T(8,128)S(1)} %get-tuple-element.35.refs_0_), channel_id=1, source_target_pairs={{0,2},{1,3},{2,0},{3,1},{4,6},{5,7},{6,4},{7,5},{8,10},{9,11},{10,... | collective-permute-start | bytes 245768 | tf_op jit(solution)/shard_map/ppermute | solution.py:522
  22.6 5.5 %collective-permute-start.5 = (f32[32,640]{1,0:T(8,128)S(1)}, f32[32,640]{1,0:T(8,128)S(1)}, u32[]{:S(2)}, u32[]{:S(2)}) collective-permute-start(f32[32,640]{1,0:T(8,128)S(1)} %get-tuple-element.35.refs_0_), channel_id=1, source_target_pairs={{0,3},{1,0},{2,1},{3,2},{4,7},{5,4},{6,5},{7,6},{8,11},{9,8},{10,9... | collective-permute-start | bytes 245768 | tf_op jit(solution)/shard_map/ppermute | solution.py:522
  33.4 2.6 %collective-permute-start.7 = (f32[256,512]{1,0:T(8,128)S(1)}, f32[256,512]{1,0:T(8,128)S(1)}, u32[]{:S(2)}, u32[]{:S(2)}) collective-permute-start(f32[256,512]{1,0:T(8,128)S(1)} %get-tuple-element.43), channel_id=1, source_target_pairs={{0,4},{4,0},{8,12},{12,8},{16,20},{20,16},{24,28},{28,24},{1,5},{5... | collective-permute-start | bytes 1572872 | tf_op jit(solution)/shard_map/ppermute | solution.py:541
  33.5 1.9 %collective-permute-start.6 = (f32[3,256]{1,0:T(4,128)S(1)}, f32[3,256]{1,0:T(4,128)S(1)}, u32[]{:S(2)}, u32[]{:S(2)}) collective-permute-start(f32[3,256]{1,0:T(4,128)S(1)} %slice.19), channel_id=1, source_target_pairs={{0,4},{4,0},{8,12},{12,8},{16,20},{20,16},{24,28},{28,24},{1,5},{5... | collective-permute-start | bytes 9224 | tf_op jit(solution)/shard_map/ppermute | solution.py:542

commit v3 on v2

--- a/solution.py
+++ b/solution.py
@@ -45,6 +45,12 @@
 
 def softplus(x):
     return jnp.maximum(x, 0.0) + jnp.log1p(jnp.exp(-jnp.abs(x)))
+
+
+def partner(slab, k, slabs):
+    if slabs & (slabs - 1) == 0:
+        return slab ^ k
+    return (slab - k + slabs) % slabs
 
 
 def swap(x):
@@ -283,7 +289,11 @@
     chans = slope_ref.shape[1] // 8
     own_width = grad_ref.shape[1]
     second = lax.broadcasted_iota(jnp.int32, (8, width), 0) >= 4
-    loads = [pltpu.make_async_copy(away_ref.at[k], slope_ref.at[k], sems.at[k]) for k in range(inner)]
+    cuts = (0, inner // 3, 2 * inner // 3, inner)
+    loads = [
+        pltpu.make_async_copy(away_ref.at[a:b], slope_ref.at[a:b], sems.at[i])
+        for i, (a, b) in enumerate(zip(cuts, cuts[1:]))
+    ]
     for load in loads:
         load.start()
 
@@ -299,7 +309,7 @@
         colours.append((c0, c1, c2))
         here = (ref[16:24, :], ref[24:32, :])
         hits = here if hits is None else (hits[0] + here[0], hits[1] + here[1])
-    index = [lax.rem(slab - k + slabs, slabs) for k in range(slabs)]
+    index = [partner(slab, k, slabs) for k in range(slabs)]
     full = [jnp.zeros((8, width), F32) for _ in range(3)]
     after = [jnp.zeros((8, width), F32) for _ in range(3)]
     prefix = None
@@ -376,8 +386,8 @@
         colour_ref[o : o + 1, :] = jnp.sum(found[4 * o : 4 * o + 4], axis=0, keepdims=True)
 
     def pair(k):
-        if 0 < k < last:
-            loads[k - 1].wait()
+        if k - 1 in cuts[:-1]:
+            loads[cuts.index(k - 1)].wait()
         slope = slope_ref[k - 1] if 0 < k < last else slope2_ref[k // last]
         grad_features = jnp.dot(point_ref[...], thirds(e_ref[k]), preferred_element_type=F32)
         gdw_ref[k] = (grad_features * slope).astype(BF16)
@@ -473,14 +483,11 @@
         far=(0, 1, 2),
     )
 
-    masks = [split << k for k in range((views // split).bit_length() - 1)]
-    blocks = two[chans:, :count]
-    one = send(one, masks[0] if masks else 0, lambda s: (s + 1 - 2 * (s % 2)) % slabs)
-    one, wide = lax.optimization_barrier((one, wide))
-    if masks:
-        two = lax.dynamic_update_slice(two, one[chans:, :count], (chans, count))
-        blocks = two[chans:, : 2 * count]
-    two = send(two, masks[1] if len(masks) > 1 else 0, lambda s: (s + 2 * (s % 2) - 1) % slabs)
+    chips = views // split
+    blocks = [one[chans:, :count]]
+    one = send(one, split if chips > 1 else 0, lambda s: (s + 1 - 2 * (s % 2)) % slabs)
+    two = send(two, 2 * split if chips > 2 else 0, lambda s: (s + 2 * (s % 2) - 1) % slabs)
+    rest = [send(blocks[0], m * split, lambda s: s) for m in range(3, chips)]
     inner = depth - 1
     slope, raw, edge = call(
         inner_kernel,
@@ -494,11 +501,9 @@
         0,
         away_out=0,
     )
-    two, raw, edge = lax.optimization_barrier((two, raw, edge))
-    if len(masks) > 1:
-        blocks = jnp.concatenate([blocks, two[chans:, : 2 * count]], axis=1)
-    for mask in masks[2:]:
-        blocks = jnp.concatenate([blocks, send(blocks, mask, lambda s: s)], axis=1)
+    one, two, rest, raw, edge = lax.optimization_barrier((one, two, rest, raw, edge))
+    blocks += [one[chans:, :count], two[chans:, :count]][: chips - 1]
+    blocks = jnp.concatenate(blocks + rest, axis=1)
     groups = [blocks]
     if split == 2:
         pairing = [(i, i ^ 1) for i in range(views)]
@@ -519,7 +524,7 @@
     )
     messages = [message]
     for k in range(1, slabs):
-        messages.append(lax.ppermute(message, "slab", [(i, (i + k) % slabs) for i in range(slabs)]))
+        messages.append(lax.ppermute(message, "slab", [(partner(i, k, slabs), i) for i in range(slabs)]))
     grad, found = call(
         functools.partial(back_kernel, scale),
         [((chans * depth, own_width), F32), ((3, split * count), F32)],

time: 37.4 us -> 36.7 us (0.981)
  starting transfers between devices: 13 us -> 11.9 us
  waiting for transfers between devices: 5.28 us -> 5.74 us
    ppermute x2 -> x3, starting transfers between devices: 8.9 us -> 7.75 us  [send(): return lax.ppermute(x, ('view', 'slab'), pairs)]
    ppermute x3, waiting for transfers between devices: 3.42 us -> 4.32 us  [on_device(): lax.ppermute(message, 'slab', [(partner(i, k, slabs), i) for i in range(s...]
    ppermute x2 -> x3, waiting for transfers between devices: 0.45 us -> 0.01 us  [send(): return lax.ppermute(x, ('view', 'slab'), pairs)]
  transfers between devices with their start and end apart: 8 -> 9, of which waited for: 4 -> 3; matrix products, arithmetic and copies ran while one was open for 2% -> 2% of each run, Pallas kernels for 20% -> 20%
where the time goes in v3:
time: 36.7 us; the launch traced here: 36.4 us
  Pallas kernels  15 us (41%)
  starting transfers between devices  11.9 us (32%)
  waiting for transfers between devices  5.74 us (16%)
  local copies, waits for them, and re-layouts  1.69 us (5%)
  other arithmetic  1.24 us (3%)
  between operations  0.8 us (2%)
    pallas_call x6, Pallas kernels, call(): pl.pallas_call(kernel, out_shape=shapes, in_specs=specs, out_specs=out_sp...  15 us
    ppermute x3, starting transfers between devices, send(): return lax.ppermute(x, ('view', 'slab'), pairs)  7.75 us
    ppermute x3, waiting for transfers between devices, on_device(): lax.ppermute(message, 'slab', [(partner(i, k, slabs), i) for i in range(s...  4.32 us
    ppermute x3, starting transfers between devices, on_device(): lax.ppermute(message, 'slab', [(partner(i, k, slabs), i) for i in range(s...  3.55 us
    unnamed x4, local copies, waits for them, and re-layouts  1.64 us
    ppermute x1, waiting for transfers between devices, on_device(): colour = colour + lax.ppermute(found[:, count:], 'view', pairing)  1.4 us
    select_n x1, other arithmetic, on_device(): jnp.where(half == 0, jnp.concatenate([grad, other], axis=1), jnp.concaten...  1.15 us
  transfers between devices with their start and end apart: 9, of which 3 were waited for; matrix products, arithmetic and copies ran while one was open for 2% of the time, Pallas kernels for 20%

profile of v3, /device:TPU:0, one launch (start us, length us, event | category | flops | bytes accessed | tf_op | source)
XLA Modules:
  0.0 36.4 jit_solution(4686193922503971861)
XLA Ops:
  0.6 0.0 copy-start
  0.7 1.0 %copy-done = bf16[32,8,1024]{2,1,0:T(8,128)(2,1)S(1)} copy-done((bf16[32,8,1024]{2,1,0:T(8,128)(2,1)S(1)}, bf16[32,8,1024]{2,1,0:T(8,128)(2,1)}, u32[]{:S(2)}) %copy-start) | copy-done | bytes 524312
  1.8 0.1 pad_add_fusion.where_ref
  1.8 0.7 %shard_map.77 = (bf16[48,640]{1,0:T(8,128)(2,1)S(1)}, bf16[48,640]{1,0:T(8,128)(2,1)S(1)}) custom-call(s32[4]{0:T(128)S(1)} %pad_add_fusion.where_ref, bf16[8,32,640]{2,1,0:T(8,128)(2,1)S(1)} %bitcast.12, f32[3,1,256]{2,1,0:T(1,128)} %bitcast.17, s32[1,1024]{1,0:T(1,128)} %ids_ref.1), custom_call_target="tpu_custom_call" | custom-call | tf_op jit(solution)/shard_map/pallas_call | solution.py:434
  2.6 4.0 %collective-permute-start = (bf16[48,640]{1,0:T(8,128)(2,1)S(1)}, bf16[48,640]{1,0:T(8,128)(2,1)S(1)}, u32[]{:S(2)}, u32[]{:S(2)}) collective-permute-start(bf16[48,640]{1,0:T(8,128)(2,1)S(1)} %get-tuple-element.23), channel_id=1, source_target_pairs={{0,9},{1,8},{2,11},{3,10},{4,13},{5,12},{6,15},{7,14},{8,1},{9,0},... | collective-permute-start | bytes 184328 | tf_op jit(solution)/shard_map/ppermute | solution.py:470
  6.6 3.5 %collective-permute-start.1 = (bf16[48,640]{1,0:T(8,128)(2,1)S(1)}, bf16[48,640]{1,0:T(8,128)(2,1)S(1)}, u32[]{:S(2)}, u32[]{:S(2)}) collective-permute-start(bf16[48,640]{1,0:T(8,128)(2,1)S(1)} %get-tuple-element.24), channel_id=1, source_target_pairs={{0,19},{1,18},{2,17},{3,16},{4,23},{5,22},{6,21},{7,20},{8,27},{9,... | collective-permute-start | bytes 184328 | tf_op jit(solution)/shard_map/ppermute | solution.py:470
  10.1 0.2 collective-permute-start.2
  10.4 1.7 %shard_map.78 = (bf16[4,128,256]{2,1,0:T(8,128)(2,1)S(1)}, bf16[2,192,256]{2,1,0:T(8,128)(2,1)S(1)}, bf16[32,256]{1,0:T(8,128)(2,1)S(1)}, bf16[256,96]{1,0:T(8,128)(2,1)S(1)}) custom-call(bf16[32,8,32]{2,1,0:T(8,128)(2,1)} %bitcast.16, f32[32,27]{1,0:T(8,128)} %depth_ref.1, bf16[4,32]{1,0:T(4,128)(2,1)} %weight_ref.1), custom_call_target="tpu_custom_call" | custom-call | tf_op jit(solution)/shard_map/pallas_call | solution.py:434
  12.1 3.9 %shard_map.79 = (f32[7,256,640]{2,1,0:T(8,128)}, f32[7,32,640]{2,1,0:T(8,128)S(1)}, bf16[2,288,640]{2,1,0:T(8,128)(2,1)S(1)}) custom-call(bf16[8,32,640]{2,1,0:T(8,128)(2,1)S(1)} %bitcast.13, bf16[4,128,256]{2,1,0:T(8,128)(2,1)S(1)} %get-tuple-element.25.wide_ref, bf16[32,256]{1,0:T(8,128)(2,1)S(1)} %get-tuple-element.26.point_ref), custom_call_target="tpu_custom_call" | custom-call | tf_op jit(solution)/shard_map/pallas_call | solution.py:434
  16.1 0.0 collective-permute-done.2
  16.1 0.1 collective-permute-start.3
  16.2 1.7 %shard_map.80 = (f32[2,256,640]{2,1,0:T(8,128)S(1)}, f32[2,32,640]{2,1,0:T(8,128)S(1)}, f32[16,640]{1,0:T(8,128)S(1)}) custom-call(s32[4]{0:T(128)S(1)} %pad_add_fusion.where_ref, bf16[48,640]{1,0:T(8,128)(2,1)S(1)} %collective-permute-done.one_ref, bf16[48,640]{1,0:T(8,128)(2,1)S(1)} %collective-permute-done.1.two_ref, ...), custom_call_target="tpu_custom_call" | custom-call | tf_op jit(solution)/shard_map/pallas_call | solution.py:434
  17.9 1.6 %shard_map.81 = (f32[32,640]{1,0:T(8,128)S(1)}, s32[1,512]{1,0:T(1,128)S(1)}) custom-call(s32[4]{0:T(128)S(1)} %pad_add_fusion.where_ref, f32[16,640]{1,0:T(8,128)S(1)} %get-tuple-element.33.tot_ref, bf16[16,1024]{1,0:T(8,128)(2,1)S(1)} %pad_maximum_fusion.refs_0_, bf16[16,1024]{1,0:T(8,128)(2,1)S(1)} %collective-permute-done.3.refs_1_), custom_call_target="tpu_custom_call" | custom-call | tf_op jit(solution)/shard_map/pallas_call | solution.py:434
  19.5 1.6 %collective-permute-start.4 = (f32[32,640]{1,0:T(8,128)S(1)}, f32[32,640]{1,0:T(8,128)S(1)}, u32[]{:S(2)}, u32[]{:S(2)}) collective-permute-start(f32[32,640]{1,0:T(8,128)S(1)} %get-tuple-element.35.refs_0_), channel_id=1, source_target_pairs={{1,0},{0,1},{3,2},{2,3},{5,4},{4,5},{7,6},{6,7},{9,8},{8,9},{11,10... | collective-permute-start | bytes 245768 | tf_op jit(solution)/shard_map/ppermute | solution.py:527
  21.1 0.5 %collective-permute-start.5 = (f32[32,640]{1,0:T(8,128)S(1)}, f32[32,640]{1,0:T(8,128)S(1)}, u32[]{:S(2)}, u32[]{:S(2)}) collective-permute-start(f32[32,640]{1,0:T(8,128)S(1)} %get-tuple-element.35.refs_0_), channel_id=1, source_target_pairs={{2,0},{3,1},{0,2},{1,3},{6,4},{7,5},{4,6},{5,7},{10,8},{11,9},{8,1... | collective-permute-start | bytes 245768 | tf_op jit(solution)/shard_map/ppermute | solution.py:527
  21.6 1.5 %collective-permute-start.6 = (f32[32,640]{1,0:T(8,128)S(1)}, f32[32,640]{1,0:T(8,128)S(1)}, u32[]{:S(2)}, u32[]{:S(2)}) collective-permute-start(f32[32,640]{1,0:T(8,128)S(1)} %get-tuple-element.35.refs_0_), channel_id=1, source_target_pairs={{3,0},{2,1},{1,2},{0,3},{7,4},{6,5},{5,6},{4,7},{11,8},{10,9},{9,1... | collective-permute-start | bytes 245768 | tf_op jit(solution)/shard_map/ppermute | solution.py:527
  23.1 1.4 %collective-permute-done.4.refs_1_ = f32[32,640]{1,0:T(8,128)S(1)} collective-permute-done((f32[32,640]{1,0:T(8,128)S(1)}, f32[32,640]{1,0:T(8,128)S(1)}, u32[]{:S(2)}, u32[]{:S(2)}) %collective-permute-start.4) | collective-permute-done | bytes 81952 | tf_op jit(solution)/shard_map/ppermute | solution.py:527
  24.4 3.0 %collective-permute-done.5.refs_2_ = f32[32,640]{1,0:T(8,128)S(1)} collective-permute-done((f32[32,640]{1,0:T(8,128)S(1)}, f32[32,640]{1,0:T(8,128)S(1)}, u32[]{:S(2)}, u32[]{:S(2)}) %collective-permute-start.5) | collective-permute-done | bytes 81952 | tf_op jit(solution)/shard_map/ppermute | solution.py:527
  27.4 5.3 %shard_map.82 = (f32[256,512]{1,0:T(8,128)S(1)}, f32[3,512]{1,0:T(4,128)S(1)}) custom-call(s32[4]{0:T(128)S(1)} %pad_add_fusion.where_ref, f32[32,640]{1,0:T(8,128)S(1)} %get-tuple-element.35.refs_0_, f32[32,640]{1,0:T(8,128)S(1)} %collective-permute-done.4.refs_1_, f32[32,640]{1,0:T(8,128)S(1)} %collective-permute-done.5.refs_2_, ...), custom_call_target="tpu_custom_call" | custom-call | tf_op jit(solution)/shard_map/pallas_call | solution.py:434
  32.7 0.1 collective-permute-start.8
  32.8 0.5 %collective-permute-start.7 = (f32[3,256]{1,0:T(4,128)S(1)}, f32[3,256]{1,0:T(4,128)S(1)}, u32[]{:S(2)}, u32[]{:S(2)}) collective-permute-start(f32[3,256]{1,0:T(4,128)S(1)} %slice.19), channel_id=1, source_target_pairs={{0,4},{4,0},{8,12},{12,8},{16,20},{20,16},{24,28},{28,24},{1,5},{5... | collective-permute-start | bytes 9224 | tf_op jit(solution)/shard_map/ppermute | solution.py:547
  33.3 1.4 %collective-permute-done.7 = f32[3,256]{1,0:T(4,128)S(1)} collective-permute-done((f32[3,256]{1,0:T(4,128)S(1)}, f32[3,256]{1,0:T(4,128)S(1)}, u32[]{:S(2)}, u32[]{:S(2)}) %collective-permute-start.7) | collective-permute-done | bytes 3104 | tf_op jit(solution)/shard_map/ppermute | solution.py:547
  34.7 0.6 %copy.9 = f32[1,3,256]{2,0,1:T(1,128)} copy(f32[1,3,256]{2,1,0:T(4,128)S(1)} %add_bitcast_fusion) | data formatting | bytes 6144
  35.3 1.1 %maximum_select_fusion = f32[32,8,1024]{2,1,0:T(8,128)} fusion(f32[32,8,512]{2,1,0:T(8,128)S(1)} %bitcast.15, f32[32,8,512]{2,1,0:T(8,128)S(1)} %bitcast.14, pred[]{:T(512)S(6)} %eq.5), kind=kLoop, calls=%fused_computation | loop fusion | flops 786432 | bytes 2097153 | tf_op jit(solution)/shard_map/jit(_where)/select_n | solution.py:548
  (13 shorter events, 0.1 us)
Async XLA Ops:
  0.6 1.0 %copy-start = (bf16[32,8,1024]{2,1,0:T(8,128)(2,1)S(1)}, bf16[32,8,1024]{2,1,0:T(8,128)(2,1)}, u32[]{:S(2)}) copy-start(bf16[32,8,1024]{2,1,0:T(8,128)(2,1)} %param.6) | copy-start | bytes 1572868
  2.6 13.5 %collective-permute-start = (bf16[48,640]{1,0:T(8,128)(2,1)S(1)}, bf16[48,640]{1,0:T(8,128)(2,1)S(1)}, u32[]{:S(2)}, u32[]{:S(2)}) collective-permute-start(bf16[48,640]{1,0:T(8,128)(2,1)S(1)} %get-tuple-element.23), channel_id=1, source_target_pairs={{0,9},{1,8},{2,11},{3,10},{4,13},{5,12},{6,15},{7,14},{8,1},{9,0},... | collective-permute-start | bytes 184328 | tf_op jit(solution)/shard_map/ppermute | solution.py:470
  6.6 9.5 %collective-permute-start.1 = (bf16[48,640]{1,0:T(8,128)(2,1)S(1)}, bf16[48,640]{1,0:T(8,128)(2,1)S(1)}, u32[]{:S(2)}, u32[]{:S(2)}) collective-permute-start(bf16[48,640]{1,0:T(8,128)(2,1)S(1)} %get-tuple-element.24), channel_id=1, source_target_pairs={{0,19},{1,18},{2,17},{3,16},{4,23},{5,22},{6,21},{7,20},{8,27},{9,... | collective-permute-start | bytes 184328 | tf_op jit(solution)/shard_map/ppermute | solution.py:470
  10.1 5.9 %collective-permute-start.2 = (bf16[16,256]{1,0:T(8,128)(2,1)S(1)}, bf16[16,256]{1,0:T(8,128)(2,1)S(1)}, u32[]{:S(2)}, u32[]{:S(2)}) collective-permute-start(bf16[16,256]{1,0:T(8,128)(2,1)S(1)} %slice.15), channel_id=1, source_target_pairs={{0,24},{1,25},{2,26},{3,27},{4,28},{5,29},{6,30},{7,31},{8,16},{9,... | collective-permute-start | bytes 24584 | tf_op jit(solution)/shard_map/ppermute | solution.py:470
  16.1 1.8 %collective-permute-start.3 = (bf16[16,1024]{1,0:T(8,128)(2,1)S(1)}, bf16[16,1024]{1,0:T(8,128)(2,1)S(1)}, u32[]{:S(2)}, u32[]{:S(2)}) collective-permute-start(bf16[16,1024]{1,0:T(8,128)(2,1)S(1)} %pad_maximum_fusion.refs_0_), channel_id=1, source_target_pairs={{0,4},{4,0},{8,12},{12,8},{16,20},{20,16},{24,28},{28,24},{1,5},{5... | collective-permute-start | bytes 98312 | tf_op jit(solution)/shard_map/ppermute | solution.py:510
  19.5 4.9 %collective-permute-start.4 = (f32[32,640]{1,0:T(8,128)S(1)}, f32[32,640]{1,0:T(8,128)S(1)}, u32[]{:S(2)}, u32[]{:S(2)}) collective-permute-start(f32[32,640]{1,0:T(8,128)S(1)} %get-tuple-element.35.refs_0_), channel_id=1, source_target_pairs={{1,0},{0,1},{3,2},{2,3},{5,4},{4,5},{7,6},{6,7},{9,8},{8,9},{11,10... | collective-permute-start | bytes 245768 | tf_op jit(solution)/shard_map/ppermute | solution.py:527
  21.1 6.3 %collective-permute-start.5 = (f32[32,640]{1,0:T(8,128)S(1)}, f32[32,640]{1,0:T(8,128)S(1)}, u32[]{:S(2)}, u32[]{:S(2)}) collective-permute-start(f32[32,640]{1,0:T(8,128)S(1)} %get-tuple-element.35.refs_0_), channel_id=1, source_target_pairs={{2,0},{3,1},{0,2},{1,3},{6,4},{7,5},{4,6},{5,7},{10,8},{11,9},{8,1... | collective-permute-start | bytes 245768 | tf_op jit(solution)/shard_map/ppermute | solution.py:527
  21.6 5.8 %collective-permute-start.6 = (f32[32,640]{1,0:T(8,128)S(1)}, f32[32,640]{1,0:T(8,128)S(1)}, u32[]{:S(2)}, u32[]{:S(2)}) collective-permute-start(f32[32,640]{1,0:T(8,128)S(1)} %get-tuple-element.35.refs_0_), channel_id=1, source_target_pairs={{3,0},{2,1},{1,2},{0,3},{7,4},{6,5},{5,6},{4,7},{11,8},{10,9},{9,1... | collective-permute-start | bytes 245768 | tf_op jit(solution)/shard_map/ppermute | solution.py:527
  32.7 2.6 %collective-permute-start.8 = (f32[256,512]{1,0:T(8,128)S(1)}, f32[256,512]{1,0:T(8,128)S(1)}, u32[]{:S(2)}, u32[]{:S(2)}) collective-permute-start(f32[256,512]{1,0:T(8,128)S(1)} %get-tuple-element.43), channel_id=1, source_target_pairs={{0,4},{4,0},{8,12},{12,8},{16,20},{20,16},{24,28},{28,24},{1,5},{5... | collective-permute-start | bytes 1572872 | tf_op jit(solution)/shard_map/ppermute | solution.py:546
  32.8 1.9 %collective-permute-start.7 = (f32[3,256]{1,0:T(4,128)S(1)}, f32[3,256]{1,0:T(4,128)S(1)}, u32[]{:S(2)}, u32[]{:S(2)}) collective-permute-start(f32[3,256]{1,0:T(4,128)S(1)} %slice.19), channel_id=1, source_target_pairs={{0,4},{4,0},{8,12},{12,8},{16,20},{20,16},{24,28},{28,24},{1,5},{5... | collective-permute-start | bytes 9224 | tf_op jit(solution)/shard_map/ppermute | solution.py:547

commit v4 on v3

--- a/solution.py
+++ b/solution.py
@@ -113,15 +113,27 @@
     raw_ref[k] = jnp.dot(point, jnp.concatenate(features, axis=0), preferred_element_type=F32)
 
 
-def weight_kernel(
-    tconv_ref, depth_ref, weight_ref, wide_ref, turned_ref, point_ref, back_ref,
-    taps_ref, depth_pad_ref, full_ref, full2_ref,
-):
+def taps_and_depth(tconv_ref, depth_ref, taps_ref, depth_pad_ref):
     chans = tconv_ref.shape[0]
     taps_ref[:, 0:chans] = tconv_ref[...].astype(F32).reshape(8 * chans, chans)
     taps = [taps_ref[pl.ds(q, chans, stride=8), :][:, :chans] for q in range(8)]
     depth_pad_ref[:, 0:27] = depth_ref[...]
-    depth = depth_pad_ref[...].T
+    return taps, depth_pad_ref[...].T
+
+
+def point_lines(weight_ref):
+    chans = weight_ref.shape[1]
+    weight = weight_ref[...].astype(F32)
+    lines = jnp.concatenate([weight] * 8, axis=1)
+    lines = jnp.concatenate([jnp.broadcast_to(lines[o : o + 1], (8, 8 * chans)) for o in range(4)], axis=0)
+    row = lax.broadcasted_iota(jnp.int32, lines.shape, 0) % 8
+    col = lax.broadcasted_iota(jnp.int32, lines.shape, 1) // chans
+    return jnp.where(col == 2 * (row % 4) + row // 4, lines, 0.0)
+
+
+def weight_kernel(tconv_ref, depth_ref, weight_ref, wide_ref, point_ref, taps_ref, depth_pad_ref, full_ref):
+    chans = tconv_ref.shape[0]
+    taps, depth = taps_and_depth(tconv_ref, depth_ref, taps_ref, depth_pad_ref)
     for b in range(2):
         for c in range(2):
             for first in range(2):
@@ -136,6 +148,12 @@
             high = whole.astype(BF16)
             wide_ref[2 * b + c, : 2 * chans, :] = high
             wide_ref[2 * b + c, 2 * chans :, :] = (whole - high.astype(F32)).astype(BF16)
+    point_ref[...] = point_lines(weight_ref).astype(BF16)
+
+
+def turn_kernel(tconv_ref, depth_ref, weight_ref, _, turned_ref, back_ref, taps_ref, depth_pad_ref, full2_ref):
+    chans = tconv_ref.shape[0]
+    taps, depth = taps_and_depth(tconv_ref, depth_ref, taps_ref, depth_pad_ref)
     full2_ref[...] = jnp.zeros_like(full2_ref)
     for b in range(2):
         for n in range(2):
@@ -149,14 +167,7 @@
                             col = chans * (4 * (j // 2) + 2 * c + j % 2)
                             full2_ref[b, row : row + chans, col : col + chans] = composed(taps, depth, e)
     turned_ref[...] = full2_ref[...].astype(BF16)
-    weight = weight_ref[...].astype(F32)
-    lines = jnp.concatenate([weight] * 8, axis=1)
-    lines = jnp.concatenate([jnp.broadcast_to(lines[o : o + 1], (8, 8 * chans)) for o in range(4)], axis=0)
-    row = lax.broadcasted_iota(jnp.int32, lines.shape, 0) % 8
-    col = lax.broadcasted_iota(jnp.int32, lines.shape, 1) // chans
-    lines = jnp.where(col == 2 * (row % 4) + row // 4, lines, 0.0)
-    point_ref[...] = lines.astype(BF16)
-    turned = lines.T
+    turned = point_lines(weight_ref).T
     back_ref[...] = jnp.concatenate([turned] * 3, axis=1).astype(BF16)
 
 
@@ -469,16 +480,13 @@
         pairs = [(v * slabs + s, (v ^ mask) * slabs + partner(s)) for v in range(views) for s in range(slabs)]
         return lax.ppermute(x, ("view", "slab"), pairs)
 
-    wide, turned, point, point_back = call(
+    small = (jnp.transpose(tconv_weight, (0, 2, 1)), depth_weight, point_weight)
+    room = [((8 * chans, 128), F32), ((chans, 128), F32)]
+    wide, point = call(
         weight_kernel,
-        [
-            ((4, 4 * chans, 8 * chans), BF16),
-            ((2, 6 * chans, 8 * chans), BF16),
-            ((32, 8 * chans), BF16),
-            ((8 * chans, 96), BF16),
-        ],
-        [((8 * chans, 128), F32), ((chans, 128), F32), ((4, 8 * chans, 128), F32), ((2, 6 * chans, 8 * chans), F32)],
-        (jnp.transpose(tconv_weight, (0, 2, 1)), depth_weight, point_weight),
+        [((4, 4 * chans, 8 * chans), BF16), ((32, 8 * chans), BF16)],
+        [*room, ((4, 8 * chans, 128), F32)],
+        small,
         0,
         far=(0, 1, 2),
     )
@@ -525,6 +533,14 @@
     messages = [message]
     for k in range(1, slabs):
         messages.append(lax.ppermute(message, "slab", [(partner(i, k, slabs), i) for i in range(slabs)]))
+    turned, point_back = call(
+        turn_kernel,
+        [((2, 6 * chans, 8 * chans), BF16), ((8 * chans, 96), BF16)],
+        [*room, ((2, 6 * chans, 8 * chans), F32)],
+        (*small, message),
+        0,
+        far=(0, 1, 2),
+    )
     grad, found = call(
         functools.partial(back_kernel, scale),
         [((chans * depth, own_width), F32), ((3, split * count), F32)],

time: 36.7 us -> 36.4 us (level)
  waiting for transfers between devices: 5.74 us -> 4.22 us
  Pallas kernels: 15 us -> 16.2 us
    ppermute x3, waiting for transfers between devices: 4.32 us -> 2.8 us  [on_device(): lax.ppermute(message, 'slab', [(partner(i, k, slabs), i) for i in range(s...]
    pallas_call x6 -> x7, Pallas kernels: 15 us -> 16.2 us  [call(): pl.pallas_call(kernel, out_shape=shapes, in_specs=specs, out_specs=out_sp...]
  transfers between devices with their start and end apart: 9 -> 9, of which waited for: 3 -> 2; matrix products, arithmetic and copies ran while one was open for 2% -> 2% of each run, Pallas kernels for 20% -> 23%
where the time goes in v4:
time: 36.4 us; the launch traced here: 36.1 us
  Pallas kernels  16.2 us (45%)
  starting transfers between devices  11.9 us (33%)
  waiting for transfers between devices  4.22 us (12%)
  local copies, waits for them, and re-layouts  1.69 us (5%)
  other arithmetic  1.24 us (3%)
  between operations  0.81 us (2%)
    pallas_call x7, Pallas kernels, call(): pl.pallas_call(kernel, out_shape=shapes, in_specs=specs, out_specs=out_sp...  16.2 us
    ppermute x3, starting transfers between devices, send(): return lax.ppermute(x, ('view', 'slab'), pairs)  7.75 us
    ppermute x3, starting transfers between devices, on_device(): lax.ppermute(message, 'slab', [(partner(i, k, slabs), i) for i in range(s...  3.55 us
    ppermute x3, waiting for transfers between devices, on_device(): lax.ppermute(message, 'slab', [(partner(i, k, slabs), i) for i in range(s...  2.8 us
    unnamed x4, local copies, waits for them, and re-layouts  1.64 us
    ppermute x1, waiting for transfers between devices, on_device(): colour = colour + lax.ppermute(found[:, count:], 'view', pairing)  1.4 us
    select_n x1, other arithmetic, on_device(): jnp.where(half == 0, jnp.concatenate([grad, other], axis=1), jnp.concaten...  1.15 us
  transfers between devices with their start and end apart: 9, of which 2 were waited for; matrix products, arithmetic and copies ran while one was open for 2% of the time, Pallas kernels for 23%

profile of v4, /device:TPU:0, one launch (start us, length us, event | category | flops | bytes accessed | tf_op | source)
XLA Modules:
  0.0 36.1 jit_solution(17603411129578374064)
XLA Ops:
  0.6 0.0 copy-start
  0.7 1.0 %copy-done = bf16[32,8,1024]{2,1,0:T(8,128)(2,1)S(1)} copy-done((bf16[32,8,1024]{2,1,0:T(8,128)(2,1)S(1)}, bf16[32,8,1024]{2,1,0:T(8,128)(2,1)}, u32[]{:S(2)}) %copy-start) | copy-done | bytes 524312
  1.8 0.1 pad_add_fusion.where_ref
  1.8 0.7 %shard_map.77 = (bf16[48,640]{1,0:T(8,128)(2,1)S(1)}, bf16[48,640]{1,0:T(8,128)(2,1)S(1)}) custom-call(s32[4]{0:T(128)S(1)} %pad_add_fusion.where_ref, bf16[8,32,640]{2,1,0:T(8,128)(2,1)S(1)} %bitcast.12, f32[3,1,256]{2,1,0:T(1,128)} %bitcast.18, s32[1,1024]{1,0:T(1,128)} %ids_ref.1), custom_call_target="tpu_custom_call" | custom-call | tf_op jit(solution)/shard_map/pallas_call | solution.py:445
  2.6 4.0 %collective-permute-start = (bf16[48,640]{1,0:T(8,128)(2,1)S(1)}, bf16[48,640]{1,0:T(8,128)(2,1)S(1)}, u32[]{:S(2)}, u32[]{:S(2)}) collective-permute-start(bf16[48,640]{1,0:T(8,128)(2,1)S(1)} %get-tuple-element.23), channel_id=1, source_target_pairs={{0,9},{1,8},{2,11},{3,10},{4,13},{5,12},{6,15},{7,14},{8,1},{9,0},... | collective-permute-start | bytes 184328 | tf_op jit(solution)/shard_map/ppermute | solution.py:481
  6.6 3.5 %collective-permute-start.1 = (bf16[48,640]{1,0:T(8,128)(2,1)S(1)}, bf16[48,640]{1,0:T(8,128)(2,1)S(1)}, u32[]{:S(2)}, u32[]{:S(2)}) collective-permute-start(bf16[48,640]{1,0:T(8,128)(2,1)S(1)} %get-tuple-element.24), channel_id=1, source_target_pairs={{0,19},{1,18},{2,17},{3,16},{4,23},{5,22},{6,21},{7,20},{8,27},{9,... | collective-permute-start | bytes 184328 | tf_op jit(solution)/shard_map/ppermute | solution.py:481
  10.1 0.2 collective-permute-start.2
  10.4 1.3 %shard_map.78 = (bf16[4,128,256]{2,1,0:T(8,128)(2,1)S(1)}, bf16[32,256]{1,0:T(8,128)(2,1)S(1)}) custom-call(bf16[32,8,32]{2,1,0:T(8,128)(2,1)} %bitcast.16, f32[32,27]{1,0:T(8,128)} %depth_ref.3, bf16[4,32]{1,0:T(4,128)(2,1)} %weight_ref.3), custom_call_target="tpu_custom_call" | custom-call | tf_op jit(solution)/shard_map/pallas_call | solution.py:445
  11.7 4.0 %shard_map.79 = (f32[7,256,640]{2,1,0:T(8,128)}, f32[7,32,640]{2,1,0:T(8,128)S(1)}, bf16[2,288,640]{2,1,0:T(8,128)(2,1)S(1)}) custom-call(bf16[8,32,640]{2,1,0:T(8,128)(2,1)S(1)} %bitcast.13, bf16[4,128,256]{2,1,0:T(8,128)(2,1)S(1)} %get-tuple-element.25.wide_ref, bf16[32,256]{1,0:T(8,128)(2,1)S(1)} %get-tuple-element.26.point_ref), custom_call_target="tpu_custom_call" | custom-call | tf_op jit(solution)/shard_map/pallas_call | solution.py:445
  15.7 0.0 collective-permute-done.2
  15.7 0.1 collective-permute-start.3
  15.8 1.7 %shard_map.80 = (f32[2,256,640]{2,1,0:T(8,128)S(1)}, f32[2,32,640]{2,1,0:T(8,128)S(1)}, f32[16,640]{1,0:T(8,128)S(1)}) custom-call(s32[4]{0:T(128)S(1)} %pad_add_fusion.where_ref, bf16[48,640]{1,0:T(8,128)(2,1)S(1)} %collective-permute-done.one_ref, bf16[48,640]{1,0:T(8,128)(2,1)S(1)} %collective-permute-done.1.two_ref, ...), custom_call_target="tpu_custom_call" | custom-call | tf_op jit(solution)/shard_map/pallas_call | solution.py:445
  17.5 1.6 %shard_map.81 = (f32[32,640]{1,0:T(8,128)S(1)}, s32[1,512]{1,0:T(1,128)S(1)}) custom-call(s32[4]{0:T(128)S(1)} %pad_add_fusion.where_ref, f32[16,640]{1,0:T(8,128)S(1)} %get-tuple-element.33.tot_ref, bf16[16,1024]{1,0:T(8,128)(2,1)S(1)} %pad_maximum_fusion.refs_0_, bf16[16,1024]{1,0:T(8,128)(2,1)S(1)} %collective-permute-done.3.refs_1_), custom_call_target="tpu_custom_call" | custom-call | tf_op jit(solution)/shard_map/pallas_call | solution.py:445
  19.2 1.6 %collective-permute-start.4 = (f32[32,640]{1,0:T(8,128)S(1)}, f32[32,640]{1,0:T(8,128)S(1)}, u32[]{:S(2)}, u32[]{:S(2)}) collective-permute-start(f32[32,640]{1,0:T(8,128)S(1)} %get-tuple-element.35._.refs_0_), channel_id=1, source_target_pairs={{1,0},{0,1},{3,2},{2,3},{5,4},{4,5},{7,6},{6,7},{9,8},{8,9},{11,10... | collective-permute-start | bytes 245768 | tf_op jit(solution)/shard_map/ppermute | solution.py:535
  20.7 0.5 %collective-permute-start.5 = (f32[32,640]{1,0:T(8,128)S(1)}, f32[32,640]{1,0:T(8,128)S(1)}, u32[]{:S(2)}, u32[]{:S(2)}) collective-permute-start(f32[32,640]{1,0:T(8,128)S(1)} %get-tuple-element.35._.refs_0_), channel_id=1, source_target_pairs={{2,0},{3,1},{0,2},{1,3},{6,4},{7,5},{4,6},{5,7},{10,8},{11,9},{8,1... | collective-permute-start | bytes 245768 | tf_op jit(solution)/shard_map/ppermute | solution.py:535
  21.2 1.5 %collective-permute-start.6 = (f32[32,640]{1,0:T(8,128)S(1)}, f32[32,640]{1,0:T(8,128)S(1)}, u32[]{:S(2)}, u32[]{:S(2)}) collective-permute-start(f32[32,640]{1,0:T(8,128)S(1)} %get-tuple-element.35._.refs_0_), channel_id=1, source_target_pairs={{3,0},{2,1},{1,2},{0,3},{7,4},{6,5},{5,6},{4,7},{11,8},{10,9},{9,1... | collective-permute-start | bytes 245768 | tf_op jit(solution)/shard_map/ppermute | solution.py:535
  22.7 1.5 %shard_map.82 = (bf16[2,192,256]{2,1,0:T(8,128)(2,1)S(1)}, bf16[256,96]{1,0:T(8,128)(2,1)S(1)}) custom-call(bf16[32,8,32]{2,1,0:T(8,128)(2,1)} %bitcast.17, f32[32,27]{1,0:T(8,128)} %depth_ref.3, bf16[4,32]{1,0:T(4,128)(2,1)} %weight_ref.3, f32[32,640]{1,0:T(8,128)S(1)} %get-tuple-element.35._.refs_0_), custom_call_target="tpu_custom_call" | custom-call | tf_op jit(solution)/shard_map/pallas_call | solution.py:445
  24.2 2.8 %collective-permute-done.5.refs_2_ = f32[32,640]{1,0:T(8,128)S(1)} collective-permute-done((f32[32,640]{1,0:T(8,128)S(1)}, f32[32,640]{1,0:T(8,128)S(1)}, u32[]{:S(2)}, u32[]{:S(2)}) %collective-permute-start.5) | collective-permute-done | bytes 81952 | tf_op jit(solution)/shard_map/ppermute | solution.py:535
  27.0 5.3 %shard_map.83 = (f32[256,512]{1,0:T(8,128)S(1)}, f32[3,512]{1,0:T(4,128)S(1)}) custom-call(s32[4]{0:T(128)S(1)} %pad_add_fusion.where_ref, f32[32,640]{1,0:T(8,128)S(1)} %get-tuple-element.35._.refs_0_, f32[32,640]{1,0:T(8,128)S(1)} %collective-permute-done.4.refs_1_, f32[32,640]{1,0:T(8,128)S(1)} %collective-permute-done.5.refs_2_, ...), custom_call_target="tpu_custom_call" | custom-call | tf_op jit(solution)/shard_map/pallas_call | solution.py:445
  32.4 0.1 collective-permute-start.8
  32.5 0.5 %collective-permute-start.7 = (f32[3,256]{1,0:T(4,128)S(1)}, f32[3,256]{1,0:T(4,128)S(1)}, u32[]{:S(2)}, u32[]{:S(2)}) collective-permute-start(f32[3,256]{1,0:T(4,128)S(1)} %slice.19), channel_id=1, source_target_pairs={{0,4},{4,0},{8,12},{12,8},{16,20},{20,16},{24,28},{28,24},{1,5},{5... | collective-permute-start | bytes 9224 | tf_op jit(solution)/shard_map/ppermute | solution.py:563
  32.9 1.4 %collective-permute-done.7 = f32[3,256]{1,0:T(4,128)S(1)} collective-permute-done((f32[3,256]{1,0:T(4,128)S(1)}, f32[3,256]{1,0:T(4,128)S(1)}, u32[]{:S(2)}, u32[]{:S(2)}) %collective-permute-start.7) | collective-permute-done | bytes 3104 | tf_op jit(solution)/shard_map/ppermute | solution.py:563
  34.4 0.6 %copy.9 = f32[1,3,256]{2,0,1:T(1,128)} copy(f32[1,3,256]{2,1,0:T(4,128)S(1)} %add_bitcast_fusion) | data formatting | bytes 6144
  34.9 1.1 %maximum_select_fusion = f32[32,8,1024]{2,1,0:T(8,128)} fusion(f32[32,8,512]{2,1,0:T(8,128)S(1)} %bitcast.15, f32[32,8,512]{2,1,0:T(8,128)S(1)} %bitcast.14, pred[]{:T(512)S(6)} %eq.5), kind=kLoop, calls=%fused_computation | loop fusion | flops 786432 | bytes 2097153 | tf_op jit(solution)/shard_map/jit(_where)/select_n | solution.py:564
  (14 shorter events, 0.1 us)
Async XLA Ops:
  0.6 1.0 %copy-start = (bf16[32,8,1024]{2,1,0:T(8,128)(2,1)S(1)}, bf16[32,8,1024]{2,1,0:T(8,128)(2,1)}, u32[]{:S(2)}) copy-start(bf16[32,8,1024]{2,1,0:T(8,128)(2,1)} %param.6) | copy-start | bytes 1572868
  2.6 13.1 %collective-permute-start = (bf16[48,640]{1,0:T(8,128)(2,1)S(1)}, bf16[48,640]{1,0:T(8,128)(2,1)S(1)}, u32[]{:S(2)}, u32[]{:S(2)}) collective-permute-start(bf16[48,640]{1,0:T(8,128)(2,1)S(1)} %get-tuple-element.23), channel_id=1, source_target_pairs={{0,9},{1,8},{2,11},{3,10},{4,13},{5,12},{6,15},{7,14},{8,1},{9,0},... | collective-permute-start | bytes 184328 | tf_op jit(solution)/shard_map/ppermute | solution.py:481
  6.6 9.1 %collective-permute-start.1 = (bf16[48,640]{1,0:T(8,128)(2,1)S(1)}, bf16[48,640]{1,0:T(8,128)(2,1)S(1)}, u32[]{:S(2)}, u32[]{:S(2)}) collective-permute-start(bf16[48,640]{1,0:T(8,128)(2,1)S(1)} %get-tuple-element.24), channel_id=1, source_target_pairs={{0,19},{1,18},{2,17},{3,16},{4,23},{5,22},{6,21},{7,20},{8,27},{9,... | collective-permute-start | bytes 184328 | tf_op jit(solution)/shard_map/ppermute | solution.py:481
  10.1 5.5 %collective-permute-start.2 = (bf16[16,256]{1,0:T(8,128)(2,1)S(1)}, bf16[16,256]{1,0:T(8,128)(2,1)S(1)}, u32[]{:S(2)}, u32[]{:S(2)}) collective-permute-start(bf16[16,256]{1,0:T(8,128)(2,1)S(1)} %slice.15), channel_id=1, source_target_pairs={{0,24},{1,25},{2,26},{3,27},{4,28},{5,29},{6,30},{7,31},{8,16},{9,... | collective-permute-start | bytes 24584 | tf_op jit(solution)/shard_map/ppermute | solution.py:481
  15.7 1.8 %collective-permute-start.3 = (bf16[16,1024]{1,0:T(8,128)(2,1)S(1)}, bf16[16,1024]{1,0:T(8,128)(2,1)S(1)}, u32[]{:S(2)}, u32[]{:S(2)}) collective-permute-start(bf16[16,1024]{1,0:T(8,128)(2,1)S(1)} %pad_maximum_fusion.refs_0_), channel_id=1, source_target_pairs={{0,4},{4,0},{8,12},{12,8},{16,20},{20,16},{24,28},{28,24},{1,5},{5... | collective-permute-start | bytes 98312 | tf_op jit(solution)/shard_map/ppermute | solution.py:518
  19.2 5.1 %collective-permute-start.4 = (f32[32,640]{1,0:T(8,128)S(1)}, f32[32,640]{1,0:T(8,128)S(1)}, u32[]{:S(2)}, u32[]{:S(2)}) collective-permute-start(f32[32,640]{1,0:T(8,128)S(1)} %get-tuple-element.35._.refs_0_), channel_id=1, source_target_pairs={{1,0},{0,1},{3,2},{2,3},{5,4},{4,5},{7,6},{6,7},{9,8},{8,9},{11,10... | collective-permute-start | bytes 245768 | tf_op jit(solution)/shard_map/ppermute | solution.py:535
  20.7 6.3 %collective-permute-start.5 = (f32[32,640]{1,0:T(8,128)S(1)}, f32[32,640]{1,0:T(8,128)S(1)}, u32[]{:S(2)}, u32[]{:S(2)}) collective-permute-start(f32[32,640]{1,0:T(8,128)S(1)} %get-tuple-element.35._.refs_0_), channel_id=1, source_target_pairs={{2,0},{3,1},{0,2},{1,3},{6,4},{7,5},{4,6},{5,7},{10,8},{11,9},{8,1... | collective-permute-start | bytes 245768 | tf_op jit(solution)/shard_map/ppermute | solution.py:535
  21.2 5.8 %collective-permute-start.6 = (f32[32,640]{1,0:T(8,128)S(1)}, f32[32,640]{1,0:T(8,128)S(1)}, u32[]{:S(2)}, u32[]{:S(2)}) collective-permute-start(f32[32,640]{1,0:T(8,128)S(1)} %get-tuple-element.35._.refs_0_), channel_id=1, source_target_pairs={{3,0},{2,1},{1,2},{0,3},{7,4},{6,5},{5,6},{4,7},{11,8},{10,9},{9,1... | collective-permute-start | bytes 245768 | tf_op jit(solution)/shard_map/ppermute | solution.py:535
  32.4 2.6 %collective-permute-start.8 = (f32[256,512]{1,0:T(8,128)S(1)}, f32[256,512]{1,0:T(8,128)S(1)}, u32[]{:S(2)}, u32[]{:S(2)}) collective-permute-start(f32[256,512]{1,0:T(8,128)S(1)} %get-tuple-element.43), channel_id=1, source_target_pairs={{0,4},{4,0},{8,12},{12,8},{16,20},{20,16},{24,28},{28,24},{1,5},{5... | collective-permute-start | bytes 1572872 | tf_op jit(solution)/shard_map/ppermute | solution.py:562
  32.5 1.9 %collective-permute-start.7 = (f32[3,256]{1,0:T(4,128)S(1)}, f32[3,256]{1,0:T(4,128)S(1)}, u32[]{:S(2)}, u32[]{:S(2)}) collective-permute-start(f32[3,256]{1,0:T(4,128)S(1)} %slice.19), channel_id=1, source_target_pairs={{0,4},{4,0},{8,12},{12,8},{16,20},{20,16},{24,28},{28,24},{1,5},{5... | collective-permute-start | bytes 9224 | tf_op jit(solution)/shard_map/ppermute | solution.py:563

commit v5 on v4

--- a/solution.py
+++ b/solution.py
@@ -192,7 +192,7 @@
     return x[0:4] + x[4:8] + x[8:12]
 
 
-def inner_kernel(lat_ref, wide_ref, point_ref, away_ref, raw_ref, edge_ref, x9_ref, slope_ref, sems):
+def inner_kernel(lat_ref, wide_ref, point_ref, away_ref, raw_ref, edge_ref, near_ref, x9_ref, slope_ref, sems):
     layers, chans, width = lat_ref.shape
 
 
@@ -207,10 +207,12 @@
         layer(k + 1)
         around = [lambda at, j=j: x9_ref[k + j, at : at + chans, :] for j in range(2)]
         decode_pair(around, wide_ref, point_ref[...], slope_ref, raw_ref, k)
-        pltpu.make_async_copy(slope_ref.at[k], away_ref.at[k], sems.at[k]).start()
+        if k < layers - 2:
+            pltpu.make_async_copy(slope_ref.at[k], away_ref.at[k], sems.at[k]).start()
     edge_ref[0] = x9_ref[0]
     edge_ref[1] = x9_ref[layers - 1]
-    for k in range(layers - 1):
+    near_ref[...] = slope_ref[layers - 2]
+    for k in range(layers - 2):
         pltpu.make_async_copy(slope_ref.at[k], away_ref.at[k], sems.at[k]).wait()
 
 
@@ -291,7 +293,7 @@
 
 
 def back_kernel(scale, where_ref, *refs):
-    (*msg_refs, inner_ref, outer_ref, away_ref, slope2_ref, wide_ref, point_ref, near_ref) = refs[:-8]
+    (*msg_refs, inner_ref, outer_ref, away_ref, slope2_ref, wide_ref, point_ref, near_ref, slope3_ref) = refs[:-8]
     grad_ref, colour_ref, gdw_ref, e_ref, w_ref, tile_ref, slope_ref, sems = refs[-8:]
     slab, start, own_start = where_ref[0], where_ref[1], where_ref[2]
     slabs = len(msg_refs)
@@ -300,7 +302,7 @@
     chans = slope_ref.shape[1] // 8
     own_width = grad_ref.shape[1]
     second = lax.broadcasted_iota(jnp.int32, (8, width), 0) >= 4
-    cuts = (0, inner // 3, 2 * inner // 3, inner)
+    cuts = (0, (inner - 1) // 3, 2 * (inner - 1) // 3, inner - 1)
     loads = [
         pltpu.make_async_copy(away_ref.at[a:b], slope_ref.at[a:b], sems.at[i])
         for i, (a, b) in enumerate(zip(cuts, cuts[1:]))
@@ -399,13 +401,13 @@
     def pair(k):
         if k - 1 in cuts[:-1]:
             loads[cuts.index(k - 1)].wait()
-        slope = slope_ref[k - 1] if 0 < k < last else slope2_ref[k // last]
+        slope = slope3_ref[...] if k == inner else slope_ref[k - 1] if 0 < k < last else slope2_ref[k // last]
         grad_features = jnp.dot(point_ref[...], thirds(e_ref[k]), preferred_element_type=F32)
         gdw_ref[k] = (grad_features * slope).astype(BF16)
 
     y = lax.broadcasted_iota(jnp.int32, (chans, width), 1) % CY
     low = own_start == start
-    for k in (0, last, *range(1, last)):
+    for k in (0, last, inner, *range(1, inner)):
         pair(k)
     for z in range(pairs - 1):
         every = []
@@ -497,9 +499,14 @@
     two = send(two, 2 * split if chips > 2 else 0, lambda s: (s + 2 * (s % 2) - 1) % slabs)
     rest = [send(blocks[0], m * split, lambda s: s) for m in range(3, chips)]
     inner = depth - 1
-    slope, raw, edge = call(
+    slope, raw, edge, slope3 = call(
         inner_kernel,
-        [((inner, 8 * chans, width), F32), ((inner, 32, width), F32), ((2, 9 * chans, width), BF16)],
+        [
+            ((inner - 1, 8 * chans, width), F32),
+            ((inner, 32, width), F32),
+            ((2, 9 * chans, width), BF16),
+            ((8 * chans, width), F32),
+        ],
         [
             ((depth, 9 * chans, width), BF16),
             ((inner, 8 * chans, width), F32),
@@ -531,8 +538,9 @@
         1,
     )
     messages = [message]
-    for k in range(1, slabs):
-        messages.append(lax.ppermute(message, "slab", [(partner(i, k, slabs), i) for i in range(slabs)]))
+    for k in range(slabs - 1, 0, -1):
+        sent = lax.ppermute(message, "slab", [(partner(i, k, slabs), i) for i in range(slabs)])
+        messages.insert(1, sent)
     turned, point_back = call(
         turn_kernel,
         [((2, 6 * chans, 8 * chans), BF16), ((8 * chans, 96), BF16)],
@@ -549,10 +557,10 @@
             ((inner + 2, 32, width), F32),
             ((inner + 2, 16, width), F32),
             ((own_width // 128, chans * depth, 128), F32),
-            ((inner, 8 * chans, width), F32),
+            ((inner - 1, 8 * chans, width), F32),
             pltpu.SemaphoreType.DMA((inner,)),
         ],
-        (where, *messages, raw, raw2, slope, slope2, turned, point_back, near_ids),
+        (where, *messages, raw, raw2, slope, slope2, turned, point_back, near_ids, slope3),
         1,
         far=(slabs + 3,),
         away=(slabs + 3,),

time: 36.4 us -> 36.5 us (level)
  transfers between devices with their start and end apart: 9 -> 9, of which waited for: 2 -> 3; matrix products, arithmetic and copies ran while one was open for 2% -> 2% of each run, Pallas kernels for 23% -> 22%
where the time goes in v5:
time: 36.5 us; the launch traced here: 36.2 us
  Pallas kernels  16 us (44%)
  starting transfers between devices  11.9 us (33%)
  waiting for transfers between devices  4.54 us (12%)
  local copies, waits for them, and re-layouts  1.69 us (5%)
  other arithmetic  1.24 us (3%)
  between operations  0.79 us (2%)
    pallas_call x7, Pallas kernels, call(): pl.pallas_call(kernel, out_shape=shapes, in_specs=specs, out_specs=out_sp...  16 us
    ppermute x3, starting transfers between devices, send(): return lax.ppermute(x, ('view', 'slab'), pairs)  7.75 us
    ppermute x3, starting transfers between devices, on_device(): lax.ppermute(message, 'slab', [(partner(i, k, slabs), i) for i in range(s...  3.55 us
    ppermute x3, waiting for transfers between devices, on_device(): lax.ppermute(message, 'slab', [(partner(i, k, slabs), i) for i in range(s...  2.81 us
    unnamed x4, local copies, waits for them, and re-layouts  1.64 us
    ppermute x1, waiting for transfers between devices, on_device(): colour = colour + lax.ppermute(found[:, count:], 'view', pairing)  1.4 us
    select_n x1, other arithmetic, on_device(): jnp.where(half == 0, jnp.concatenate([grad, other], axis=1), jnp.concaten...  1.15 us
  transfers between devices with their start and end apart: 9, of which 3 were waited for; matrix products, arithmetic and copies ran while one was open for 2% of the time, Pallas kernels for 22%

profile of v5, /device:TPU:0, one launch (start us, length us, event | category | flops | bytes accessed | tf_op | source)
XLA Modules:
  0.0 36.2 jit_solution(6828413159159732803)
XLA Ops:
  0.6 0.0 copy-start
  0.7 1.0 %copy-done = bf16[32,8,1024]{2,1,0:T(8,128)(2,1)S(1)} copy-done((bf16[32,8,1024]{2,1,0:T(8,128)(2,1)S(1)}, bf16[32,8,1024]{2,1,0:T(8,128)(2,1)}, u32[]{:S(2)}) %copy-start) | copy-done | bytes 524312
  1.8 0.1 pad_add_fusion.where_ref
  1.8 0.7 %shard_map.77 = (bf16[48,640]{1,0:T(8,128)(2,1)S(1)}, bf16[48,640]{1,0:T(8,128)(2,1)S(1)}) custom-call(s32[4]{0:T(128)S(1)} %pad_add_fusion.where_ref, bf16[8,32,640]{2,1,0:T(8,128)(2,1)S(1)} %bitcast.12, f32[3,1,256]{2,1,0:T(1,128)} %bitcast.18, s32[1,1024]{1,0:T(1,128)} %ids_ref.1), custom_call_target="tpu_custom_call" | custom-call | tf_op jit(solution)/shard_map/pallas_call | solution.py:447
  2.6 4.0 %collective-permute-start = (bf16[48,640]{1,0:T(8,128)(2,1)S(1)}, bf16[48,640]{1,0:T(8,128)(2,1)S(1)}, u32[]{:S(2)}, u32[]{:S(2)}) collective-permute-start(bf16[48,640]{1,0:T(8,128)(2,1)S(1)} %get-tuple-element.24), channel_id=1, source_target_pairs={{0,9},{1,8},{2,11},{3,10},{4,13},{5,12},{6,15},{7,14},{8,1},{9,0},... | collective-permute-start | bytes 184328 | tf_op jit(solution)/shard_map/ppermute | solution.py:483
  6.6 3.5 %collective-permute-start.1 = (bf16[48,640]{1,0:T(8,128)(2,1)S(1)}, bf16[48,640]{1,0:T(8,128)(2,1)S(1)}, u32[]{:S(2)}, u32[]{:S(2)}) collective-permute-start(bf16[48,640]{1,0:T(8,128)(2,1)S(1)} %get-tuple-element.25), channel_id=1, source_target_pairs={{0,19},{1,18},{2,17},{3,16},{4,23},{5,22},{6,21},{7,20},{8,27},{9,... | collective-permute-start | bytes 184328 | tf_op jit(solution)/shard_map/ppermute | solution.py:483
  10.1 0.2 collective-permute-start.2
  10.4 1.3 %shard_map.78 = (bf16[4,128,256]{2,1,0:T(8,128)(2,1)S(1)}, bf16[32,256]{1,0:T(8,128)(2,1)S(1)}) custom-call(bf16[32,8,32]{2,1,0:T(8,128)(2,1)} %bitcast.16, f32[32,27]{1,0:T(8,128)} %depth_ref.3, bf16[4,32]{1,0:T(4,128)(2,1)} %weight_ref.3), custom_call_target="tpu_custom_call" | custom-call | tf_op jit(solution)/shard_map/pallas_call | solution.py:447
  11.7 3.6 %shard_map.79 = (f32[6,256,640]{2,1,0:T(8,128)}, f32[7,32,640]{2,1,0:T(8,128)S(1)}, bf16[2,288,640]{2,1,0:T(8,128)(2,1)S(1)}, f32[256,640]{1,0:T(8,128)S(1)}) custom-call(bf16[8,32,640]{2,1,0:T(8,128)(2,1)S(1)} %bitcast.13, bf16[4,128,256]{2,1,0:T(8,128)(2,1)S(1)} %get-tuple-element.26.wide_ref, bf16[32,256]{1,0:T(8,128)(2,1)S(1)} %get-tuple-element.27.point_ref), custom_call_target="tpu_custom_call" | custom-call | tf_op jit(solution)/shard_map/pallas_call | solution.py:447
  15.3 0.3 collective-permute-done.2
  15.6 0.1 collective-permute-start.3
  15.7 1.7 %shard_map.80 = (f32[2,256,640]{2,1,0:T(8,128)S(1)}, f32[2,32,640]{2,1,0:T(8,128)S(1)}, f32[16,640]{1,0:T(8,128)S(1)}) custom-call(s32[4]{0:T(128)S(1)} %pad_add_fusion.where_ref, bf16[48,640]{1,0:T(8,128)(2,1)S(1)} %collective-permute-done.one_ref, bf16[48,640]{1,0:T(8,128)(2,1)S(1)} %collective-permute-done.1.two_ref, ...), custom_call_target="tpu_custom_call" | custom-call | tf_op jit(solution)/shard_map/pallas_call | solution.py:447
  17.4 1.6 %shard_map.81 = (f32[32,640]{1,0:T(8,128)S(1)}, s32[1,512]{1,0:T(1,128)S(1)}) custom-call(s32[4]{0:T(128)S(1)} %pad_add_fusion.where_ref, f32[16,640]{1,0:T(8,128)S(1)} %get-tuple-element.34.tot_ref, bf16[16,1024]{1,0:T(8,128)(2,1)S(1)} %pad_maximum_fusion.refs_0_, bf16[16,1024]{1,0:T(8,128)(2,1)S(1)} %collective-permute-done.3.refs_1_), custom_call_target="tpu_custom_call" | custom-call | tf_op jit(solution)/shard_map/pallas_call | solution.py:447
  19.0 1.6 %collective-permute-start.4 = (f32[32,640]{1,0:T(8,128)S(1)}, f32[32,640]{1,0:T(8,128)S(1)}, u32[]{:S(2)}, u32[]{:S(2)}) collective-permute-start(f32[32,640]{1,0:T(8,128)S(1)} %get-tuple-element.36._.refs_0_), channel_id=1, source_target_pairs={{1,0},{0,1},{3,2},{2,3},{5,4},{4,5},{7,6},{6,7},{9,8},{8,9},{11,10... | collective-permute-start | bytes 245768 | tf_op jit(solution)/shard_map/ppermute | solution.py:542
  20.6 0.5 %collective-permute-start.5 = (f32[32,640]{1,0:T(8,128)S(1)}, f32[32,640]{1,0:T(8,128)S(1)}, u32[]{:S(2)}, u32[]{:S(2)}) collective-permute-start(f32[32,640]{1,0:T(8,128)S(1)} %get-tuple-element.36._.refs_0_), channel_id=1, source_target_pairs={{2,0},{3,1},{0,2},{1,3},{6,4},{7,5},{4,6},{5,7},{10,8},{11,9},{8,1... | collective-permute-start | bytes 245768 | tf_op jit(solution)/shard_map/ppermute | solution.py:542
  21.1 1.5 %collective-permute-start.6 = (f32[32,640]{1,0:T(8,128)S(1)}, f32[32,640]{1,0:T(8,128)S(1)}, u32[]{:S(2)}, u32[]{:S(2)}) collective-permute-start(f32[32,640]{1,0:T(8,128)S(1)} %get-tuple-element.36._.refs_0_), channel_id=1, source_target_pairs={{3,0},{2,1},{1,2},{0,3},{7,4},{6,5},{5,6},{4,7},{11,8},{10,9},{9,1... | collective-permute-start | bytes 245768 | tf_op jit(solution)/shard_map/ppermute | solution.py:542
  22.6 1.5 %shard_map.82 = (bf16[2,192,256]{2,1,0:T(8,128)(2,1)S(1)}, bf16[256,96]{1,0:T(8,128)(2,1)S(1)}) custom-call(bf16[32,8,32]{2,1,0:T(8,128)(2,1)} %bitcast.17, f32[32,27]{1,0:T(8,128)} %depth_ref.3, bf16[4,32]{1,0:T(4,128)(2,1)} %weight_ref.3, f32[32,640]{1,0:T(8,128)S(1)} %get-tuple-element.36._.refs_0_), custom_call_target="tpu_custom_call" | custom-call | tf_op jit(solution)/shard_map/pallas_call | solution.py:447
  24.1 2.8 %collective-permute-done.5.refs_2_ = f32[32,640]{1,0:T(8,128)S(1)} collective-permute-done((f32[32,640]{1,0:T(8,128)S(1)}, f32[32,640]{1,0:T(8,128)S(1)}, u32[]{:S(2)}, u32[]{:S(2)}) %collective-permute-start.5) | collective-permute-done | bytes 81952 | tf_op jit(solution)/shard_map/ppermute | solution.py:542
  26.9 5.5 %shard_map.83 = (f32[256,512]{1,0:T(8,128)S(1)}, f32[3,512]{1,0:T(4,128)S(1)}) custom-call(s32[4]{0:T(128)S(1)} %pad_add_fusion.where_ref, f32[32,640]{1,0:T(8,128)S(1)} %get-tuple-element.36._.refs_0_, f32[32,640]{1,0:T(8,128)S(1)} %collective-permute-done.4.refs_1_, f32[32,640]{1,0:T(8,128)S(1)} %collective-permute-done.5.refs_2_, ...), custom_call_target="tpu_custom_call" | custom-call | tf_op jit(solution)/shard_map/pallas_call | solution.py:447
  32.4 0.1 collective-permute-start.8
  32.5 0.5 %collective-permute-start.7 = (f32[3,256]{1,0:T(4,128)S(1)}, f32[3,256]{1,0:T(4,128)S(1)}, u32[]{:S(2)}, u32[]{:S(2)}) collective-permute-start(f32[3,256]{1,0:T(4,128)S(1)} %slice.19), channel_id=1, source_target_pairs={{0,4},{4,0},{8,12},{12,8},{16,20},{20,16},{24,28},{28,24},{1,5},{5... | collective-permute-start | bytes 9224 | tf_op jit(solution)/shard_map/ppermute | solution.py:571
  33.0 1.4 %collective-permute-done.7 = f32[3,256]{1,0:T(4,128)S(1)} collective-permute-done((f32[3,256]{1,0:T(4,128)S(1)}, f32[3,256]{1,0:T(4,128)S(1)}, u32[]{:S(2)}, u32[]{:S(2)}) %collective-permute-start.7) | collective-permute-done | bytes 3104 | tf_op jit(solution)/shard_map/ppermute | solution.py:571
  34.4 0.6 %copy.9 = f32[1,3,256]{2,0,1:T(1,128)} copy(f32[1,3,256]{2,1,0:T(4,128)S(1)} %add_bitcast_fusion) | data formatting | bytes 6144
  35.0 1.1 %maximum_select_fusion = f32[32,8,1024]{2,1,0:T(8,128)} fusion(f32[32,8,512]{2,1,0:T(8,128)S(1)} %bitcast.15, f32[32,8,512]{2,1,0:T(8,128)S(1)} %bitcast.14, pred[]{:T(512)S(6)} %eq.5), kind=kLoop, calls=%fused_computation | loop fusion | flops 786432 | bytes 2097153 | tf_op jit(solution)/shard_map/jit(_where)/select_n | solution.py:572
  (14 shorter events, 0.1 us)
Async XLA Ops:
  0.6 1.0 %copy-start = (bf16[32,8,1024]{2,1,0:T(8,128)(2,1)S(1)}, bf16[32,8,1024]{2,1,0:T(8,128)(2,1)}, u32[]{:S(2)}) copy-start(bf16[32,8,1024]{2,1,0:T(8,128)(2,1)} %param.6) | copy-start | bytes 1572868
  2.6 13.0 %collective-permute-start = (bf16[48,640]{1,0:T(8,128)(2,1)S(1)}, bf16[48,640]{1,0:T(8,128)(2,1)S(1)}, u32[]{:S(2)}, u32[]{:S(2)}) collective-permute-start(bf16[48,640]{1,0:T(8,128)(2,1)S(1)} %get-tuple-element.24), channel_id=1, source_target_pairs={{0,9},{1,8},{2,11},{3,10},{4,13},{5,12},{6,15},{7,14},{8,1},{9,0},... | collective-permute-start | bytes 184328 | tf_op jit(solution)/shard_map/ppermute | solution.py:483
  6.6 9.0 %collective-permute-start.1 = (bf16[48,640]{1,0:T(8,128)(2,1)S(1)}, bf16[48,640]{1,0:T(8,128)(2,1)S(1)}, u32[]{:S(2)}, u32[]{:S(2)}) collective-permute-start(bf16[48,640]{1,0:T(8,128)(2,1)S(1)} %get-tuple-element.25), channel_id=1, source_target_pairs={{0,19},{1,18},{2,17},{3,16},{4,23},{5,22},{6,21},{7,20},{8,27},{9,... | collective-permute-start | bytes 184328 | tf_op jit(solution)/shard_map/ppermute | solution.py:483
  10.1 5.4 %collective-permute-start.2 = (bf16[16,256]{1,0:T(8,128)(2,1)S(1)}, bf16[16,256]{1,0:T(8,128)(2,1)S(1)}, u32[]{:S(2)}, u32[]{:S(2)}) collective-permute-start(bf16[16,256]{1,0:T(8,128)(2,1)S(1)} %slice.15), channel_id=1, source_target_pairs={{0,24},{1,25},{2,26},{3,27},{4,28},{5,29},{6,30},{7,31},{8,16},{9,... | collective-permute-start | bytes 24584 | tf_op jit(solution)/shard_map/ppermute | solution.py:483
  15.6 1.7 %collective-permute-start.3 = (bf16[16,1024]{1,0:T(8,128)(2,1)S(1)}, bf16[16,1024]{1,0:T(8,128)(2,1)S(1)}, u32[]{:S(2)}, u32[]{:S(2)}) collective-permute-start(bf16[16,1024]{1,0:T(8,128)(2,1)S(1)} %pad_maximum_fusion.refs_0_), channel_id=1, source_target_pairs={{0,4},{4,0},{8,12},{12,8},{16,20},{20,16},{24,28},{28,24},{1,5},{5... | collective-permute-start | bytes 98312 | tf_op jit(solution)/shard_map/ppermute | solution.py:525
  19.0 5.1 %collective-permute-start.4 = (f32[32,640]{1,0:T(8,128)S(1)}, f32[32,640]{1,0:T(8,128)S(1)}, u32[]{:S(2)}, u32[]{:S(2)}) collective-permute-start(f32[32,640]{1,0:T(8,128)S(1)} %get-tuple-element.36._.refs_0_), channel_id=1, source_target_pairs={{1,0},{0,1},{3,2},{2,3},{5,4},{4,5},{7,6},{6,7},{9,8},{8,9},{11,10... | collective-permute-start | bytes 245768 | tf_op jit(solution)/shard_map/ppermute | solution.py:542
  20.6 6.3 %collective-permute-start.5 = (f32[32,640]{1,0:T(8,128)S(1)}, f32[32,640]{1,0:T(8,128)S(1)}, u32[]{:S(2)}, u32[]{:S(2)}) collective-permute-start(f32[32,640]{1,0:T(8,128)S(1)} %get-tuple-element.36._.refs_0_), channel_id=1, source_target_pairs={{2,0},{3,1},{0,2},{1,3},{6,4},{7,5},{4,6},{5,7},{10,8},{11,9},{8,1... | collective-permute-start | bytes 245768 | tf_op jit(solution)/shard_map/ppermute | solution.py:542
  21.1 5.8 %collective-permute-start.6 = (f32[32,640]{1,0:T(8,128)S(1)}, f32[32,640]{1,0:T(8,128)S(1)}, u32[]{:S(2)}, u32[]{:S(2)}) collective-permute-start(f32[32,640]{1,0:T(8,128)S(1)} %get-tuple-element.36._.refs_0_), channel_id=1, source_target_pairs={{3,0},{2,1},{1,2},{0,3},{7,4},{6,5},{5,6},{4,7},{11,8},{10,9},{9,1... | collective-permute-start | bytes 245768 | tf_op jit(solution)/shard_map/ppermute | solution.py:542
  32.4 2.6 %collective-permute-start.8 = (f32[256,512]{1,0:T(8,128)S(1)}, f32[256,512]{1,0:T(8,128)S(1)}, u32[]{:S(2)}, u32[]{:S(2)}) collective-permute-start(f32[256,512]{1,0:T(8,128)S(1)} %get-tuple-element.45), channel_id=1, source_target_pairs={{0,4},{4,0},{8,12},{12,8},{16,20},{20,16},{24,28},{28,24},{1,5},{5... | collective-permute-start | bytes 1572872 | tf_op jit(solution)/shard_map/ppermute | solution.py:570
  32.5 1.9 %collective-permute-start.7 = (f32[3,256]{1,0:T(4,128)S(1)}, f32[3,256]{1,0:T(4,128)S(1)}, u32[]{:S(2)}, u32[]{:S(2)}) collective-permute-start(f32[3,256]{1,0:T(4,128)S(1)} %slice.19), channel_id=1, source_target_pairs={{0,4},{4,0},{8,12},{12,8},{16,20},{20,16},{24,28},{28,24},{1,5},{5... | collective-permute-start | bytes 9224 | tf_op jit(solution)/shard_map/ppermute | solution.py:571
